TPU v7x, 512 devices: a whole 4x8x8 slice. The times are simulated.
512 devices in a mesh: lat: 128 (over y, z, core), lon: 4 (over x).
Axes of the slice: x: 4, y: 8, z: 8, core: 2. Of those that a mesh axis runs over, the one named last changes fastest.
Arguments:
- fields: bfloat16 [1, 512, 64, 1440], P(None, 'lat', None, 'lon'), may hold values from -6 to 6
- filter_weights: bfloat16 [49, 64, 8], replicated, may hold values from -2 to 2
- filter_values: float32 [512, 49], P('lat'), may hold values from 0.03 to 0.3
- row_offsets: int32 [512, 49], P('lat'), may hold values from -3 to 3
- col_offsets: int32 [512, 49], P('lat'), may hold values from -16 to 16, as said below
- support_sizes: int32 [512], P('lat'), may hold values from 16 to 49, as said below
Outputs:
- spectrum: float32 [1, 64, 2, 256, 256], P(None, 'lon', None, 'lat')
Inputs may be any that keep to these rules, and one draw needn't show every extreme that they name: `col_offsets`: column offsets of the support lie within -16 to 16. `support_sizes`: the two latitudes nearest each pole have all 49 support cells live.
All inputs are finite; a program needn't handle non-finite values.
Results may differ from a plain program's by a relative error of at most 0.0044.
Values may be sent and summed in bfloat16 or wider, within the bound.
A program may use at most 64 MiB of HBM per device.

v0:
```python
import math

import jax
import jax.numpy as jnp
from jax import lax
from jax.sharding import PartitionSpec as P

GROUP = 8
SUPPORT = 49
LAT_REACH = 3
LON_REACH = 16
NLON = 1440
DEG = 256


def extended_2(x, sides, width, wrap):
    for axis, dim in sides:
        count, length = (lax.axis_size(axis), x.shape[dim])
        up = [(i, (i + 1) % count) for i in range(count if wrap else count - 1)]
        down = [(j, i) for i, j in up]
        last = lax.slice_in_dim(x, length - width, length, axis=dim)
        initial = lax.slice_in_dim(x, 0, width, axis=dim)
        before = lax.ppermute(last, axis, up)
        after = lax.ppermute(initial, axis, down)
        x = jnp.concatenate([before, x, after], axis=dim)
    return x


def recurrence(degree_now, orders):
    degree_square = degree_now * degree_now
    order_square = orders * orders
    active = degree_now > orders
    denominator = jnp.where(active, degree_square - order_square, 1.0)
    first_factor = jnp.sqrt((4.0 * degree_square - 1.0) / denominator)
    below = (degree_now - 1.0) * (degree_now - 1.0) - order_square
    second_factor = jnp.sqrt(
        jnp.maximum((2.0 * degree_now + 1.0) * below, 0.0)
        / (jnp.maximum(2.0 * degree_now - 3.0, 1.0) * denominator)
    )
    return (first_factor, second_factor, active)


def legendre_start(degree_count, lat_count):
    orders = jnp.arange(degree_count, dtype=jnp.float32)
    factors = jnp.arange(1, degree_count, dtype=jnp.float32)
    log_steps = jnp.log((2.0 * factors - 1.0) / (2.0 * factors))
    log_product = jnp.concatenate([jnp.zeros((1,), jnp.float32), jnp.cumsum(log_steps)])
    colatitude = math.pi * (jnp.arange(lat_count, dtype=jnp.float32) + 0.5) / lat_count
    log_sine = jnp.log(jnp.sin(colatitude))
    log_diagonal = 0.5 * (jnp.log((2.0 * orders + 1.0) / (4.0 * math.pi)) + log_product)
    diagonal_start = jnp.exp(log_diagonal[None, :] + orders[None, :] * log_sine[:, None])
    return (colatitude, diagonal_start)


def legendre_local(lat_count, degree_count, first_order, local_orders):
    colatitude, diagonal_start = legendre_start(degree_count, lat_count)
    starting = lax.dynamic_slice_in_dim(diagonal_start, first_order, local_orders, 1)
    cosine = jnp.cos(colatitude)[:, None]
    order_ints = (first_order + jnp.arange(local_orders, dtype=jnp.int32))[None, :]
    orders = order_ints.astype(jnp.float32)

    def advance(state_pair, degree_int):
        previous, before_previous = state_pair
        first_factor, second_factor, active = recurrence(degree_int.astype(jnp.float32), orders)
        fresh = jnp.where(
            active,
            first_factor * cosine * previous - second_factor * before_previous,
            jnp.where(degree_int == order_ints, starting, 0.0),
        )
        return ((fresh, previous), fresh)

    zeros_start = jnp.zeros((lat_count, local_orders), jnp.float32)
    _, table = lax.scan(
        advance, (zeros_start, zeros_start), jnp.arange(degree_count, dtype=jnp.int32), unroll=16
    )
    return (colatitude, table)


def fourier_table(lon_count, degree_count):
    columns = jnp.arange(lon_count, dtype=jnp.int32)[:, None]
    orders = jnp.arange(degree_count, dtype=jnp.int32)[None, :]
    phase = 2.0 * math.pi / lon_count * (columns * orders % lon_count).astype(jnp.float32)
    return jnp.concatenate([jnp.cos(phase), -jnp.sin(phase)], axis=1).astype(jnp.bfloat16)


def convolve(extended, effective, row_offsets, col_offsets, out_width):
    samples, padded_rows, chans, _ = extended.shape
    lat_dev = padded_rows - 2 * LAT_REACH
    groups = chans // GROUP
    lat_local = jnp.arange(lat_dev, dtype=jnp.int32)

    def pick_cell(row_start, col_start):
        return lax.dynamic_slice(
            extended, (0, row_start, 0, col_start), (samples, 1, chans, out_width)
        )[:, 0]

    pick_block = jax.vmap(jax.vmap(pick_cell))
    summed = jnp.zeros((samples, lat_dev, groups, GROUP, out_width), jnp.float32)
    per_block = 7
    for block_index in range(SUPPORT // per_block):
        low_cell = block_index * per_block
        row_start = lat_local[:, None] + LAT_REACH + row_offsets[:, low_cell : low_cell + per_block]
        col_start = LON_REACH + col_offsets[:, low_cell : low_cell + per_block]
        nearby = pick_block(row_start, col_start)
        nearby = nearby.reshape(lat_dev, per_block, samples, groups, GROUP, out_width)
        block_weight = effective[:, low_cell : low_cell + per_block].reshape(
            lat_dev, per_block, groups, GROUP, GROUP
        )
        summed = summed + jnp.einsum(
            "ikgoa,ikbgaj->bigoj", block_weight, nearby, preferred_element_type=jnp.float32
        )
    return summed.reshape(samples, lat_dev, chans, out_width).astype(jnp.bfloat16)


def body(fields, filter_weights, filter_values, row_offsets, col_offsets, support_sizes):
    samples, lat_dev, chans, lon_dev = fields.shape
    lon_parts = lax.axis_size("lon")
    lat_parts = lax.axis_size("lat")
    local_chans = chans // lon_parts
    live = (jnp.arange(SUPPORT, dtype=jnp.int32)[None, :] < support_sizes[:, None]).astype(
        jnp.float32
    )
    scaled = filter_values * live
    effective = (scaled[:, :, None, None] * filter_weights.astype(jnp.float32)[None]).astype(
        jnp.bfloat16
    )
    banded = extended_2(fields, (("lat", 1),), LAT_REACH, False)
    extended = extended_2(banded, (("lon", 3),), LON_REACH, True)
    convolved = convolve(extended, effective, row_offsets, col_offsets, lon_dev)
    strips = lax.all_to_all(convolved, "lon", split_axis=2, concat_axis=3, tiled=True)
    fourier = fourier_table(NLON, DEG)
    zonal = jnp.dot(strips.reshape(-1, NLON), fourier, preferred_element_type=jnp.float32)
    zonal = zonal.reshape(samples, lat_dev, local_chans * 2, DEG)
    lat_count = lat_dev * lat_parts
    local_orders = DEG // lat_parts
    first_order = lax.axis_index("lat") * local_orders
    colatitude, table = legendre_local(lat_count, DEG, first_order, local_orders)
    weighted = table * (math.pi / lat_count * jnp.sin(colatitude))[None, :, None]
    result = jnp.einsum(
        "lim,biqm->bqml",
        weighted,
        lax.all_to_all(zonal, "lat", split_axis=3, concat_axis=1, tiled=True),
        precision=lax.Precision.HIGHEST,
    )
    return result.reshape(samples, local_chans, 2, local_orders, DEG)


def solution(mesh):
    placed = (
        P(None, "lat", None, "lon"),
        P(),
        P("lat", None),
        P("lat", None),
        P("lat", None),
        P("lat"),
    )
    return jax.shard_map(
        body,
        mesh=mesh,
        in_specs=placed,
        out_specs=P(None, "lon", None, "lat", None),
        check_vma=False,
    )
```

profile of v0, /device:TPU:1, one launch (start us, length us, event | category | flops | bytes accessed | tf_op | source)
XLA Modules:
  0.0 576.4 jit_solution(2349363523277535409)
XLA Ops:
  1.1 5.4 collective-permute-start
  6.5 4.7 collective-permute-start.1
  11.2 7.7 %negate_convert_fusion = (bf16[1440,256]{1,0:T(8,128)(2,1)}, bf16[1440,256]{1,0:T(8,128)(2,1)}) fusion(), kind=kLoop, calls=%fused_computation.154 | loop fusion | flops 4423680 | bytes 1474560 | tf_op jit(solution)/shard_map/convert.1
  20.4 1.9 collective-permute-start.2
  22.3 4.6 collective-permute-start.3
  35.0 1.6 copy.80
  36.7 13.4 %gather_fusion = bf16[28,64,360]{1,0,2:T(8,128)(2,1)} fusion(bf16[1,10,64,392]{2,1,0,3:T(8,128)(2,1)S(1)} %copy.80, s32[28]{0:T(128)S(1)} %reshape.1255), kind=kCustom, calls=%fused_computation | custom fusion | bytes 2580928 | tf_op jit(solution)/shard_map/vmap(vmap())/gather | solution.py:93
  50.1 5.7 copy.81
  55.8 13.4 %gather_fusion.1 = bf16[28,64,360]{1,0,2:T(8,128)(2,1)} fusion(bf16[1,10,64,392]{2,1,0,3:T(8,128)(2,1)S(1)} %copy.80, s32[28]{0:T(128)S(1)} %reshape.1262), kind=kCustom, calls=%fused_computation.1 | custom fusion | bytes 2580928 | tf_op jit(solution)/shard_map/vmap(vmap())/gather | solution.py:93
  69.3 4.5 copy.85
  73.7 13.4 %gather_fusion.2 = bf16[28,64,360]{1,0,2:T(8,128)(2,1)} fusion(bf16[1,10,64,392]{2,1,0,3:T(8,128)(2,1)S(1)} %copy.80, s32[28]{0:T(128)S(1)} %reshape.1269), kind=kCustom, calls=%fused_computation.2 | custom fusion | bytes 2580928 | tf_op jit(solution)/shard_map/vmap(vmap())/gather | solution.py:93
  87.2 5.3 copy.89
  92.5 13.4 %gather_fusion.3 = bf16[28,64,360]{1,0,2:T(8,128)(2,1)} fusion(bf16[1,10,64,392]{2,1,0,3:T(8,128)(2,1)S(1)} %copy.80, s32[28]{0:T(128)S(1)} %reshape.1276), kind=kCustom, calls=%fused_computation.3 | custom fusion | bytes 2580928 | tf_op jit(solution)/shard_map/vmap(vmap())/gather | solution.py:93
  106.0 5.6 copy.93
  111.6 13.4 %gather_fusion.4 = bf16[28,64,360]{1,0,2:T(8,128)(2,1)} fusion(bf16[1,10,64,392]{2,1,0,3:T(8,128)(2,1)S(1)} %copy.80, s32[28]{0:T(128)S(1)} %reshape.1283), kind=kCustom, calls=%fused_computation.4 | custom fusion | bytes 2580928 | tf_op jit(solution)/shard_map/vmap(vmap())/gather | solution.py:93
  125.0 5.3 copy.97
  130.3 13.4 %gather_fusion.5 = bf16[28,64,360]{1,0,2:T(8,128)(2,1)} fusion(bf16[1,10,64,392]{2,1,0,3:T(8,128)(2,1)S(1)} %copy.80, s32[28]{0:T(128)S(1)} %reshape.1290), kind=kCustom, calls=%fused_computation.5 | custom fusion | bytes 2580928 | tf_op jit(solution)/shard_map/vmap(vmap())/gather | solution.py:93
  143.8 5.3 copy.101
  149.1 13.4 %gather_fusion.6 = bf16[28,64,360]{1,0,2:T(8,128)(2,1)} fusion(bf16[1,10,64,392]{2,1,0,3:T(8,128)(2,1)S(1)} %copy.80, s32[28]{0:T(128)S(1)} %reshape.1297), kind=kCustom, calls=%fused_computation.6 | custom fusion | bytes 2580928 | tf_op jit(solution)/shard_map/vmap(vmap())/gather | solution.py:93
  162.6 5.5 copy.105
  168.1 1.4 fusion.49
  176.1 3.4 all-to-all-start
  179.6 6.1 %all-to-all-done = bf16[1,4,64,360]{3,1,0,2:T(4,128)(2,1)S(1)} async-done(((bf16[1,4,64,360]{3,1,0,2:T(4,128)(2,1)}), bf16[1,4,64,360]{3,1,0,2:T(4,128)(2,1)S(1)}, u32[]{:S(2)}, u32[]{:S(2)}) %all-to-all-start) | async-done | bytes 184352 | tf_op jit(solution)/shard_map/all_to_all | solution.py:130
  187.6 15.8 %all-to-all-start.1 = ((f32[128,1,256]{2,1,0:T(1,128)}), f32[128,1,256]{2,1,0:T(1,128)S(1)}, u32[]{:S(2)}, u32[]{:S(2)}) async-start(f32[128,1,256]{2,1,0:T(1,128)} %reshape.1412), calls=%async_computation.1 | async-start | bytes 262144 | tf_op jit(solution)/shard_map/all_to_all | solution.py:142
  203.4 368.7 %while.21 = (s32[]{:T(128)}, f32[512,2]{0,1:T(2,128)S(1)}, f32[512,2]{0,1:T(2,128)S(1)}, f32[16,16,512,2]{2,3,1,0:T(2,128)S(1)}, s32[16,16]{1,0:T(8,128)S(1)}, /...) while((s32[]{:T(128)}, f32[512,2]{0,1:T(2,128)S(1)}, ...), condition=%wide.region_3.4_spmd.clone.clone.clone.clone, body=%wide.region_2.3_spmd.clone.clone.clone.clone.sunk | while | flops 103106 | bytes 527564 | solution.py:73
  208.3 1.3 compare_bitcast_fusion.57
  224.9 1.3 compare_bitcast_fusion.63
  231.4 1.3 compare_bitcast_fusion.57
  248.0 1.3 compare_bitcast_fusion.63
  254.4 1.3 compare_bitcast_fusion.57
  271.0 1.3 compare_bitcast_fusion.63
  277.4 1.3 compare_bitcast_fusion.57
  300.5 1.3 compare_bitcast_fusion.57
  323.5 1.3 compare_bitcast_fusion.57
  346.6 1.3 compare_bitcast_fusion.57
  369.6 1.3 compare_bitcast_fusion.57
  392.7 1.3 compare_bitcast_fusion.57
  415.7 1.3 compare_bitcast_fusion.57
  432.3 1.3 compare_bitcast_fusion.63
  438.7 1.3 compare_bitcast_fusion.57
  455.4 1.3 compare_bitcast_fusion.63
  461.8 1.3 compare_bitcast_fusion.57
  478.4 1.3 compare_bitcast_fusion.63
  484.8 1.3 compare_bitcast_fusion.57
  501.5 1.3 compare_bitcast_fusion.63
  507.9 1.3 compare_bitcast_fusion.57
  530.9 1.3 compare_bitcast_fusion.57
  554.0 1.3 compare_bitcast_fusion.57
  (915 shorter events, 195.8 us)
Async XLA Ops:
  0.0 18.9 %copy-start.14 = (bf16[49,64,8]{1,2,0:T(8,128)(2,1)S(1)}, bf16[49,64,8]{1,2,0:T(8,128)(2,1)}, u32[]{:S(2)}) copy-start(bf16[49,64,8]{1,2,0:T(8,128)(2,1)} %param.9) | copy-start | bytes 150532
  0.0 19.0 %copy-start.17 = (f32[4,49]{1,0:T(4,128)S(1)}, f32[4,49]{1,0:T(4,128)}, u32[]{:S(2)}) copy-start(f32[4,49]{1,0:T(4,128)} %param.10) | copy-start | bytes 2356
  0.0 19.0 %copy-start.18 = (s32[4]{0:T(128)S(1)}, s32[4]{0:T(128)}, u32[]{:S(2)}) copy-start(s32[4]{0:T(128)} %param.13) | copy-start | bytes 52
  1.1 19.1 %collective-permute-start = (bf16[1,3,64,360]{3,2,1,0:T(8,128)(2,1)S(1)}, bf16[1,3,64,360]{3,2,1,0:T(8,128)(2,1)S(1)}, u32[]{:S(2)}, u32[]{:S(2)}) collective-permute-start(bf16[1,3,64,360]{3,2,1,0:T(8,128)(2,1)S(1)} %get-tuple-element.534), channel_id=1, source_target_pairs={{0,4},{4,8},{8,12},{12,16},{16,20},{20,24},{24,28},{28,32},{32,36}... | collective-permute-start | bytes 414728 | tf_op jit(solution)/shard_map/ppermute | solution.py:23
  6.5 13.8 %collective-permute-start.1 = (bf16[1,3,64,360]{3,2,1,0:T(8,128)(2,1)S(1)}, bf16[1,3,64,360]{3,2,1,0:T(8,128)(2,1)S(1)}, u32[]{:S(2)}, u32[]{:S(2)}) collective-permute-start(bf16[1,3,64,360]{3,2,1,0:T(8,128)(2,1)S(1)} %get-tuple-element.533), channel_id=1, source_target_pairs={{4,0},{8,4},{12,8},{16,12},{20,16},{24,20},{28,24},{32,28},{36,32}... | collective-permute-start | bytes 414728 | tf_op jit(solution)/shard_map/ppermute | solution.py:24
  11.2 8.8 %copy-start.15 = (s32[4,49]{1,0:T(4,128)S(1)}, s32[4,49]{1,0:T(4,128)}, u32[]{:S(2)}) copy-start(s32[4,49]{1,0:T(4,128)} %param.12) | copy-start | bytes 2356
  11.2 8.8 %copy-start.16 = (s32[4,49]{1,0:T(4,128)S(1)}, s32[4,49]{1,0:T(4,128)}, u32[]{:S(2)}) copy-start(s32[4,49]{1,0:T(4,128)} %param.11) | copy-start | bytes 2356
  18.9 1.3 copy-start.10
  20.4 14.2 %collective-permute-start.2 = (bf16[1,10,64,16]{3,2,1,0:T(8,128)(2,1)S(1)}, bf16[1,10,64,16]{3,2,1,0:T(8,128)(2,1)S(1)}, u32[]{:S(2)}, u32[]{:S(2)}) collective-permute-start(bf16[1,10,64,16]{3,2,1,0:T(8,128)(2,1)S(1)} %get-tuple-element.524), channel_id=1, source_target_pairs={{0,1},{1,2},{2,3},{3,0},{4,5},{5,6},{6,7},{7,4},{8,9},{9,10},{10,1... | collective-permute-start | bytes 61448 | tf_op jit(solution)/shard_map/ppermute | solution.py:23
  22.3 12.2 %collective-permute-start.3 = (bf16[1,10,64,16]{3,2,1,0:T(8,128)(2,1)S(1)}, bf16[1,10,64,16]{3,2,1,0:T(8,128)(2,1)S(1)}, u32[]{:S(2)}, u32[]{:S(2)}) collective-permute-start(bf16[1,10,64,16]{3,2,1,0:T(8,128)(2,1)S(1)} %get-tuple-element.525), channel_id=1, source_target_pairs={{1,0},{2,1},{3,2},{0,3},{5,4},{6,5},{7,6},{4,7},{9,8},{10,9},{11,1... | collective-permute-start | bytes 61448 | tf_op jit(solution)/shard_map/ppermute | solution.py:24
  162.6 5.5 copy-start.8
  169.5 1.3 copy-start
  169.5 1.4 copy-start.4
  169.9 1.6 copy-start.1
  170.0 1.7 copy-start.5
  171.4 1.4 copy-start.2
  171.4 1.5 copy-start.6
  172.0 1.5 copy-start.3
  172.0 1.6 copy-start.7
  173.3 1.4 copy-start.9
  173.3 1.5 copy-start.13
  175.3 10.7 %copy-start.11 = (bf16[1440,256]{1,0:T(8,128)(2,1)S(1)}, bf16[1440,256]{1,0:T(8,128)(2,1)}, u32[]{:S(2)}) copy-start(bf16[1440,256]{1,0:T(8,128)(2,1)} %get-tuple-element.542) | copy-start | bytes 2211844
  175.3 10.7 %copy-start.12 = (bf16[1440,256]{1,0:T(8,128)(2,1)S(1)}, bf16[1440,256]{1,0:T(8,128)(2,1)}, u32[]{:S(2)}) copy-start(bf16[1440,256]{1,0:T(8,128)(2,1)} %get-tuple-element.543) | copy-start | bytes 2211844
  176.1 9.5 %all-to-all-start = ((bf16[1,4,64,360]{3,1,0,2:T(4,128)(2,1)}), bf16[1,4,64,360]{3,1,0,2:T(4,128)(2,1)S(1)}, u32[]{:S(2)}, u32[]{:S(2)}) async-start(bf16[1,4,64,360]{3,1,0,2:T(4,128)(2,1)} %copy.108), calls=%async_computation | async-start | bytes 393216 | tf_op jit(solution)/shard_map/all_to_all | solution.py:130
  187.6 384.5 %all-to-all-start.1 = ((f32[128,1,256]{2,1,0:T(1,128)}), f32[128,1,256]{2,1,0:T(1,128)S(1)}, u32[]{:S(2)}, u32[]{:S(2)}) async-start(f32[128,1,256]{2,1,0:T(1,128)} %reshape.1412), calls=%async_computation.1 | async-start | bytes 262144 | tf_op jit(solution)/shard_map/all_to_all | solution.py:142
where the time goes:
time: 585 us; the launch traced here: 576 us
  other arithmetic  200 us (34%)
  loops' own time  167 us (29%)
  local copies, waits for them, and re-layouts  161 us (28%)
  starting transfers between devices  35.7 us (6%)
  waiting for transfers between devices  6.09 us (1%)
    another operation x1, loops' own time, legendre_local(): lax.scan(advance, (zeros_start, zeros_start), jnp.arange(degree_count, dt...  167 us
    eq x128, other arithmetic, advance(): degree_int == order_ints  161 us
    gather x14, local copies, waits for them, and re-layouts, pick_cell(): lax.dynamic_slice(extended, (0, row_start, 0, col_start), (samples, 1, ch...  131 us
    while x240, other arithmetic  20.2 us
    all_to_all x1, starting transfers between devices, body(): lax.all_to_all(zonal, 'lat', split_axis=3, concat_axis=1, tiled=True)  15.8 us
  transfers between devices with their start and end apart: 6, of which 1 were waited for; matrix products, arithmetic and copies ran while one was open for 38% of the time, Pallas kernels for 0%

commit v1 on v0

v1 whole, which is shorter than its diff:
```python
import functools
import math

import jax
import jax.numpy as jnp
import ml_dtypes
import numpy as np
from jax import lax
from jax.experimental import pallas as pl
from jax.experimental.pallas import tpu as pltpu
from jax.sharding import PartitionSpec as P

GROUP = 8
SUPPORT = 49
LAT_REACH = 3
LON_REACH = 16
ROWS = 2 * LAT_REACH + 1
HALF = 64
ZC = 16
MESH = pl.DeviceIdType.MESH
NT = (((1,), (1,)), ((), ()))


def split(x):
    high = x.astype(ml_dtypes.bfloat16)
    low = (x - high.astype(np.float64)).astype(ml_dtypes.bfloat16)
    return high, low


def tables(lat_parts, lon_parts, lon_dev, lat_dev):
    nlon, nlat, deg = lon_parts * lon_dev, lat_parts * lat_dev, 2 * lat_parts
    orders = np.arange(deg)
    phase = 2.0 * math.pi / nlon * ((np.arange(nlon)[:, None] * orders[None, :]) % nlon)
    fourier = np.concatenate([np.cos(phase), -np.sin(phase)], 1).astype(ml_dtypes.bfloat16)
    fourier = fourier.reshape(lon_parts, lon_dev, 2 * deg)
    shifts = np.arange(-LON_REACH, LON_REACH + 1)
    turn = 2.0 * math.pi / nlon * ((orders[:, None] * shifts[None, :]) % nlon)
    turn = np.concatenate([np.cos(turn), np.sin(turn)], 0)
    shift_table = np.zeros((2 * deg, 2 * HALF), ml_dtypes.bfloat16)
    shift_table[:, : shifts.size], shift_table[:, HALF : HALF + shifts.size] = split(turn)
    y_count = lat_parts // ZC
    lane = np.arange(lat_parts)
    band = (lane % y_count) * ZC + lane // y_count
    lats = lat_dev * band[None, :] + (np.arange(8) % lat_dev)[:, None]
    colat = math.pi * (lats + 0.5) / nlat
    per_lat = np.stack([np.cos(colat), np.log(np.sin(colat)), math.pi / nlat * np.sin(colat)])
    factors = np.arange(1, deg)
    log_product = np.concatenate([[0.0], np.cumsum(np.log((2.0 * factors - 1) / (2.0 * factors)))])
    log_norm = 0.5 * (np.log((2.0 * orders + 1) / (4 * math.pi)) + log_product)
    grow = np.sqrt(np.maximum(4.0 * orders * orders - 1, 1.0))
    scalars = np.concatenate([grow, 1.0 / grow, log_norm])
    return fourier, shift_table, per_lat.astype(np.float32), scalars.astype(np.float32)


def kernel(
    fields, weights, values, row_off, col_off, sizes, fourier, shift_table, per_lat, scalars,
    out,
    blocks, four, shift, xs, meta_v, meta_r, meta_c, left, w, acc, z, send_a, recv_a, wide_a, send_b, recv_b,
    table, tcat,
    sem_in, sem_lon_s, sem_lon_r, sem_halo_s, sem_halo_r, sem_a_s, sem_a_r, sem_b_s, sem_b_r,
):
    lat, lon = lax.axis_index("lat"), lax.axis_index("lon")
    lat_parts, lon_parts = lax.axis_size("lat"), lax.axis_size("lon")
    y_count = lat_parts // ZC
    y, zc = lat // ZC, lat % ZC
    lat_dev, chans = blocks.shape[1], blocks.shape[2]
    deg = 2 * lat_parts
    f32, bf16 = jnp.float32, jnp.bfloat16

    barrier = pltpu.get_barrier_semaphore()
    for d in range(1, lon_parts):
        pl.semaphore_signal(barrier, 1, device_id=(lat, (lon + d) % lon_parts), device_id_type=MESH)
    for d in range(1, y_count):
        pl.semaphore_signal(
            barrier, 1, device_id=((y + d) % y_count * ZC + zc, lon), device_id_type=MESH
        )
    for d in range(1, ZC):
        pl.semaphore_signal(barrier, 1, device_id=(y * ZC + (zc + d) % ZC, lon), device_id_type=MESH)
    has_low, has_high = lat > 0, lat < lat_parts - 1

    @pl.when(has_low)
    def _():
        pl.semaphore_signal(barrier, 1, device_id=(lat - 1, lon), device_id_type=MESH)

    @pl.when(has_high)
    def _():
        pl.semaphore_signal(barrier, 1, device_id=(lat + 1, lon), device_id_type=MESH)

    get_four = pltpu.make_async_copy(fourier, four, sem_in.at[0])
    get_shift = pltpu.make_async_copy(shift_table, shift, sem_in.at[1])
    get_own = pltpu.make_async_copy(
        fields.at[:, pl.ds(lon * chans, chans), :], blocks.at[lon], sem_in.at[2]
    )
    get_own.start()
    get_shift.start()
    get_four.start()

    common = (lon_parts - 1) + (y_count - 1) + (ZC - 1)

    @pl.when(has_low & has_high)
    def _():
        pl.semaphore_wait(barrier, common + 2)

    @pl.when(jnp.logical_not(has_low & has_high))
    def _():
        pl.semaphore_wait(barrier, common + 1)

    lon_copies = []
    for d in (1, lon_parts - 1, 2):
        other = (lon + d) % lon_parts
        copy = pltpu.make_async_remote_copy(
            src_ref=fields.at[:, pl.ds(other * chans, chans), :],
            dst_ref=blocks.at[lon],
            send_sem=sem_lon_s.at[d - 1],
            recv_sem=sem_lon_r.at[d - 1],
            device_id=(lat, other),
            device_id_type=MESH,
        )
        copy.start()
        lon_copies.append((d, copy))

    cells = lax.broadcasted_iota(jnp.int32, (1, 2 * HALF), 1) % HALF
    meta_v[...] = jnp.zeros_like(meta_v)
    meta_r[...] = jnp.zeros_like(meta_r)
    meta_c[...] = jnp.zeros_like(meta_c)
    for at in (0, HALF):
        meta_v[:, at : at + SUPPORT] = values[...]
        meta_r[:, at : at + SUPPORT] = row_off[...]
        meta_c[:, at : at + SUPPORT] = col_off[...]
    get_shift.wait()
    weights_f32 = weights[...].astype(f32)
    shift_row = lax.broadcasted_iota(jnp.int32, (2 * HALF, 2 * HALF), 0)
    shift_lane = lax.broadcasted_iota(jnp.int32, (2 * HALF, 2 * HALF), 1)
    same_half = shift_row // HALF == shift_lane // HALF
    shift_of_row = shift_row % HALF - LON_REACH
    for i in range(lat_dev):
        live = (cells < sizes[i]).astype(f32)
        scaled = meta_v[i : i + 1, :] * live
        effective = (weights_f32 * scaled).astype(bf16).astype(f32)
        rows_of = meta_r[i : i + 1, :]
        for r in range(ROWS):
            left[r * 128 : (r + 1) * 128, :] = jnp.where(
                rows_of == r - LAT_REACH, effective, 0.0
            ).astype(bf16)
        pick = (same_half & (shift_of_row == meta_c[i : i + 1, :])).astype(f32).astype(bf16)
        turns = jnp.dot(shift[...], pick, preferred_element_type=f32).astype(bf16)
        w[i] = lax.dot_general(left[...], turns, NT, preferred_element_type=f32)

    def transform(block):
        data = blocks[block].reshape(lat_dev * chans, blocks.shape[3])
        part = jnp.dot(data, four[block], preferred_element_type=f32)
        return part.reshape(lat_dev, chans, 2 * deg)

    get_own.wait()
    get_four.wait()
    own = pl.ds(LAT_REACH, lat_dev)
    xs[own] = transform(lon)
    for d, copy in lon_copies:
        copy.wait_recv()
        xs[own] += transform((lon + lon_parts - d) % lon_parts)

    up = pltpu.make_async_remote_copy(
        src_ref=xs.at[pl.ds(lat_dev, LAT_REACH)],
        dst_ref=xs.at[pl.ds(0, LAT_REACH)],
        send_sem=sem_halo_s.at[0],
        recv_sem=sem_halo_r.at[0],
        device_id=((lat + 1) % lat_parts, lon),
        device_id_type=MESH,
    )
    down = pltpu.make_async_remote_copy(
        src_ref=xs.at[pl.ds(LAT_REACH, LAT_REACH)],
        dst_ref=xs.at[pl.ds(LAT_REACH + lat_dev, LAT_REACH)],
        send_sem=sem_halo_s.at[1],
        recv_sem=sem_halo_r.at[1],
        device_id=((lat + lat_parts - 1) % lat_parts, lon),
        device_id_type=MESH,
    )

    @pl.when(has_high)
    def _():
        up.start()

    @pl.when(has_low)
    def _():
        down.start()

    @pl.when(jnp.logical_not(has_low))
    def _():
        xs[0:LAT_REACH] = jnp.zeros((LAT_REACH,) + xs.shape[1:], f32)

    @pl.when(jnp.logical_not(has_high))
    def _():
        xs[LAT_REACH + lat_dev :] = jnp.zeros((LAT_REACH,) + xs.shape[1:], f32)

    groups = chans // GROUP

    def products(i, g, o, rows, x_rows):
        real = imag = None
        at = pl.multiple_of(g * (GROUP * GROUP), GROUP * GROUP) + o * GROUP
        for row, (xr, xi) in zip(rows, x_rows):
            tile = w[i, pl.ds(pl.multiple_of((row - i) * 128 + at, GROUP), GROUP), :]
            wr, wi = tile[:, :deg], tile[:, deg:]
            re, im = wr * xr - wi * xi, wr * xi + wi * xr
            real, imag = (re, im) if real is None else (real + re, imag + im)
        return real, imag

    def load_rows(rows, g):
        tiles = [xs[row, pl.ds(pl.multiple_of(g * GROUP, GROUP), GROUP), :] for row in rows]
        return [(t[:, :deg], t[:, deg:]) for t in tiles]

    def own_rows(ig, carry):
        i, g = ig // groups, ig % groups
        rows = [LAT_REACH + j for j in range(lat_dev)]
        x_rows = load_rows(rows, g)
        for o in range(GROUP):
            real, imag = products(i, g, o, rows, x_rows)
            acc[ig, o * GROUP : (o + 1) * GROUP, :deg] = real
            acc[ig, o * GROUP : (o + 1) * GROUP, deg:] = imag
        return carry

    lax.fori_loop(0, lat_dev * groups, own_rows, 0)

    @pl.when(has_low)
    def _():
        up.wait_recv()

    @pl.when(has_high)
    def _():
        down.wait_recv()

    def other_rows(ig, carry):
        i, g = ig // groups, ig % groups
        rows = [i + j + lat_dev * ((i + j) // LAT_REACH) for j in range(LAT_REACH)]
        x_rows = load_rows(rows, g)
        for o in range(GROUP):
            real, imag = products(i, g, o, rows, x_rows)
            real += acc[ig, o * GROUP : (o + 1) * GROUP, :deg]
            imag += acc[ig, o * GROUP : (o + 1) * GROUP, deg:]
            z[ig, 2 * o : 2 * o + 1, :] = jnp.sum(real, axis=0, keepdims=True)
            z[ig, 2 * o + 1 : 2 * o + 2, :] = jnp.sum(imag, axis=0, keepdims=True)
        return carry

    lax.fori_loop(0, lat_dev * groups, other_rows, 0)

    by_order = z[...].reshape(128, deg).T.astype(bf16)
    send_a[...] = by_order.reshape(y_count, 2 * ZC, 128)
    a_copies = []
    for d in range(1, y_count):
        other = (y + d) % y_count
        copy = pltpu.make_async_remote_copy(
            src_ref=send_a.at[other],
            dst_ref=recv_a.at[y],
            send_sem=sem_a_s.at[d - 1],
            recv_sem=sem_a_r.at[d - 1],
            device_id=(other * ZC + zc, lon),
            device_id_type=MESH,
        )
        copy.start()
        a_copies.append(copy)
    recv_a[y] = send_a[y]

    half = lax.broadcasted_iota(jnp.int32, (8, lat_parts), 0) // lat_dev
    orders = (2 * lat + half).astype(f32)
    order_square = orders * orders
    cosine, log_sine, weight = per_lat[0], per_lat[1], per_lat[2]
    norm = jnp.where(half == 0, scalars[2 * deg + 2 * lat], scalars[2 * deg + 2 * lat + 1])
    start = jnp.exp(norm + orders * log_sine)

    def advance(l, state):
        previous, before, inverse, degree = state
        denominator = degree * degree - order_square
        root = lax.rsqrt(jnp.maximum(denominator, 1.0))
        first = jnp.where(denominator > 0.0, scalars[l] * root, 0.0)
        second = first * inverse
        fresh = first * cosine * previous - second * before
        fresh += jnp.where(denominator == 0.0, start, 0.0)
        table[pl.ds(pl.multiple_of(l * 8, 8), 8), :] = fresh * weight
        inverse = jnp.maximum(denominator, 0.0) * root * scalars[deg + l]
        return fresh, previous, inverse, degree + 1.0

    zeros = cosine * 0.0
    lax.fori_loop(0, deg, advance, (zeros, zeros, zeros, zeros), unroll=8)

    for copy in a_copies:
        copy.wait_recv()

    wide_a[...] = recv_a[...].astype(f32).reshape(deg, 128)
    b_copies = []
    for d in range(ZC):
        other = (zc + d) % ZC
        low = wide_a[pl.ds(2 * other, y_count, stride=2 * ZC), :]
        high = wide_a[pl.ds(2 * other + 1, y_count, stride=2 * ZC), :]
        tile = jnp.concatenate([low, high], axis=0).astype(bf16)
        if d == 0:
            recv_b[zc] = tile
            continue
        send_b[other] = tile
        copy = pltpu.make_async_remote_copy(
            src_ref=send_b.at[other],
            dst_ref=recv_b.at[zc],
            send_sem=sem_b_s.at[d - 1],
            recv_sem=sem_b_r.at[d - 1],
            device_id=(y * ZC + other, lon),
            device_id_type=MESH,
        )
        copy.start()
        b_copies.append(copy)

    for s in range(8):
        exact = table[pl.ds(s, deg, stride=8), :]
        high = exact.astype(bf16)
        tcat[s, :, :lat_parts] = high
        tcat[s, :, lat_parts:] = (exact - high.astype(f32)).astype(bf16)

    for copy in b_copies:
        copy.wait_recv()

    arrived = recv_b[...].astype(f32)
    for m in range(2):
        of_order = arrived[:, m * y_count : (m + 1) * y_count, :].reshape(lat_parts, 128)
        by_lat = of_order.T.astype(bf16)
        total = None
        for i in range(lat_dev):
            part = by_lat[i * 32 : (i + 1) * 32, :]
            part = jnp.concatenate([part, part], axis=1)
            term = lax.dot_general(part, tcat[m * lat_dev + i], NT, preferred_element_type=f32)
            total = term if total is None else total + term
        out[:, m * deg : (m + 1) * deg] = total

    for _, copy in lon_copies:
        copy.wait_send()

    @pl.when(has_high)
    def _():
        up.wait_send()

    @pl.when(has_low)
    def _():
        down.wait_send()

    for copy in a_copies + b_copies:
        copy.wait_send()


def body(consts, fields, filter_weights, filter_values, row_offsets, col_offsets, support_sizes):
    _, lat_dev, all_chans, lon_dev = fields.shape
    lat_parts, lon_parts = lax.axis_size("lat"), lax.axis_size("lon")
    chans, deg, y_count = all_chans // lon_parts, 2 * lat_parts, lat_parts // ZC
    own = lax.dynamic_slice_in_dim(filter_weights, lax.axis_index("lon") * chans, chans, 1)
    own = own.transpose(1, 2, 0).reshape(chans * GROUP, SUPPORT)
    own = jnp.pad(own, ((0, 0), (0, HALF - SUPPORT)))
    own = jnp.concatenate([own, own], axis=1)
    vmem, smem = pl.BlockSpec(memory_space=pltpu.VMEM), pl.BlockSpec(memory_space=pltpu.SMEM)
    hbm = pl.BlockSpec(memory_space=pl.ANY)
    f32, bf16, dma = jnp.float32, jnp.bfloat16, pltpu.SemaphoreType.DMA
    result = pl.pallas_call(
        kernel,
        out_shape=jax.ShapeDtypeStruct((chans * 2, 2 * deg), f32),
        in_specs=[hbm, vmem, vmem, vmem, vmem, smem, hbm, hbm, vmem, smem],
        out_specs=vmem,
        scratch_shapes=[
            pltpu.VMEM((lon_parts, lat_dev, chans, lon_dev), bf16),
            pltpu.VMEM((lon_parts, lon_dev, 2 * deg), bf16),
            pltpu.VMEM((2 * deg, 2 * HALF), bf16),
            pltpu.VMEM((lat_dev + 2 * LAT_REACH, chans, 2 * deg), f32),
            pltpu.VMEM((lat_dev, 2 * HALF), f32),
            pltpu.VMEM((lat_dev, 2 * HALF), jnp.int32),
            pltpu.VMEM((lat_dev, 2 * HALF), jnp.int32),
            pltpu.VMEM((ROWS * chans * GROUP, 2 * HALF), bf16),
            pltpu.VMEM((lat_dev, ROWS * chans * GROUP, 2 * deg), f32),
            pltpu.VMEM((lat_dev * chans // GROUP, GROUP * GROUP, 2 * deg), f32),
            pltpu.VMEM((lat_dev * chans // GROUP, 2 * GROUP, deg), f32),
            pltpu.VMEM((y_count, 2 * ZC, 128), bf16),
            pltpu.VMEM((y_count, 2 * ZC, 128), bf16),
            pltpu.VMEM((deg, 128), f32),
            pltpu.VMEM((ZC, 2 * y_count, 128), bf16),
            pltpu.VMEM((ZC, 2 * y_count, 128), bf16),
            pltpu.VMEM((deg * 8, lat_parts), f32),
            pltpu.VMEM((8, deg, 2 * lat_parts), bf16),
            dma((3,)),
            dma((lon_parts - 1,)),
            dma((lon_parts - 1,)),
            dma((2,)),
            dma((2,)),
            dma((y_count - 1,)),
            dma((y_count - 1,)),
            dma((ZC - 1,)),
            dma((ZC - 1,)),
        ],
        compiler_params=pltpu.CompilerParams(
            collective_id=0, has_side_effects=True, vmem_limit_bytes=40 * 1024 * 1024
        ),
    )(
        fields[0], own, filter_values, row_offsets, col_offsets, support_sizes,
        *(jnp.asarray(c) for c in consts),
    )
    return result.reshape(1, chans, 2, 2, deg)


def solution(mesh):
    placed = (
        P(None, "lat", None, "lon"),
        P(),
        P("lat", None),
        P("lat", None),
        P("lat", None),
        P("lat"),
    )

    def whole(fields, *rest):
        lat_parts, lon_parts = mesh.shape["lat"], mesh.shape["lon"]
        consts = tables(
            lat_parts, lon_parts, fields.shape[3] // lon_parts, fields.shape[1] // lat_parts
        )
        return jax.shard_map(
            functools.partial(body, consts),
            mesh=mesh,
            in_specs=placed,
            out_specs=P(None, "lon", None, "lat", None),
            check_vma=False,
        )(fields, *rest)

    return whole
```

time: 585 us -> 47.3 us (0.08); the launches traced: 576 us -> 46.9 us
  other arithmetic: 200 us -> 0.08 us
  loops' own time: 167 us -> 0 us
  local copies, waits for them, and re-layouts: 161 us -> 9.11 us
  Pallas kernels: 0 us -> 37.7 us
  starting transfers between devices: 35.7 us -> 0 us
  waiting for transfers between devices: 6.09 us -> 0 us
    another operation x1 -> x0, loops' own time: 167 us -> none  [legendre_local(): lax.scan(advance, (zeros_start, zeros_start), jnp.arange(degree_count, dt...]
    eq x128 -> x0, other arithmetic: 161 us -> none  [advance(): degree_int == order_ints]
    gather x14 -> x0, local copies, waits for them, and re-layouts: 131 us -> none  [pick_cell(): lax.dynamic_slice(extended, (0, row_start, 0, col_start), (samples, 1, ch...]
    pallas_call x0 -> x1, Pallas kernels: none -> 37.7 us  [body(): pl.pallas_call(kernel, out_shape=jax.ShapeDtypeStruct((chans * 2, 2 * deg...]
    while x240 -> x0, other arithmetic: 20.2 us -> none
    all_to_all x2 -> x0, starting transfers between devices: 19.1 us -> none  [the longest x1 15.8 us: body(): lax.all_to_all(zonal, 'lat', split_axis=3, concat_axis=1, tiled=True)]
    ppermute x4 -> x0, starting transfers between devices: 16.6 us -> none  [the longest x2 9.26 us: extended_2(): after = lax.ppermute(initial, axis, down)]
    slice x20 -> x0, local copies, waits for them, and re-layouts: 12.8 us -> none  [the longest x16 11.5 us: legendre_local(): lax.scan(advance, (zeros_start, zeros_start), jnp.arange(degree_count, dt...]
  transfers between devices with their start and end apart: 6 -> 0, of which waited for: 1 -> 0; matrix products, arithmetic and copies ran while one was open for 38% -> 0% of each run, Pallas kernels for 0% -> 0%
where the time goes in v1:
time: 47.3 us; the launch traced here: 46.9 us
  Pallas kernels  37.7 us (80%)
  local copies, waits for them, and re-layouts  9.11 us (19%)
    pallas_call x1, Pallas kernels, body(): pl.pallas_call(kernel, out_shape=jax.ShapeDtypeStruct((chans * 2, 2 * deg...  37.7 us
    unnamed x20, local copies, waits for them, and re-layouts  8.18 us

profile of v1, /device:TPU:1, one launch (start us, length us, event | category | flops | bytes accessed | tf_op | source)
XLA Modules:
  0.0 46.9 jit_solution(16271136734566415914)
XLA Ops:
  0.0 0.0 copy-start
  0.0 0.9 %copy-done = bf16[49,64,8]{1,2,0:T(8,128)(2,1)S(1)} copy-done((bf16[49,64,8]{1,2,0:T(8,128)(2,1)S(1)}, bf16[49,64,8]{1,2,0:T(8,128)(2,1)}, u32[]{:S(2)}) %copy-start) | copy-done | bytes 50200
  0.9 0.1 dynamic-slice_bitcast_fusion
  1.0 0.2 copy.11
  1.2 0.1 pad_maximum_fusion.weights
  1.3 0.0 copy-start.1
  1.3 1.4 %copy-done.1 = bf16[4,360,512]{2,1,0:T(8,128)(2,1)S(1)} copy-done((bf16[4,360,512]{2,1,0:T(8,128)(2,1)S(1)}, bf16[4,360,512]{2,1,0:T(8,128)(2,1)}, u32[]{:S(2)}) %copy-start.1) | copy-done | bytes 1474584
  2.6 0.0 copy-start.2
  2.6 0.9 %copy-done.2 = bf16[1,4,64,360]{3,2,1,0:T(8,128)(2,1)S(1)} copy-done((bf16[1,4,64,360]{3,2,1,0:T(8,128)(2,1)S(1)}, bf16[1,4,64,360]{3,2,1,0:T(8,128)(2,1)}, u32[]{:S(2)}) %copy-start.2) | copy-done | bytes 184344
  3.6 0.0 copy-start.3
  3.6 0.9 %copy-done.3 = bf16[512,128]{1,0:T(8,128)(2,1)S(1)} copy-done((bf16[512,128]{1,0:T(8,128)(2,1)S(1)}, bf16[512,128]{1,0:T(8,128)(2,1)}, u32[]{:S(2)}) %copy-start.3) | copy-done | bytes 131096
  4.5 0.0 copy-start.4
  4.5 0.7 %copy-done.4 = f32[3,8,128]{2,1,0:T(8,128)S(1)} copy-done((f32[3,8,128]{2,1,0:T(8,128)S(1)}, f32[3,8,128]{2,1,0:T(8,128)}, u32[]{:S(2)}) %copy-start.4) | copy-done | bytes 12312
  5.2 0.0 copy-start.5
  5.2 0.7 %copy-done.5 = f32[768]{0:T(1024)S(1)} copy-done((f32[768]{0:T(1024)S(1)}, f32[768]{0:T(1024)}, u32[]{:S(2)}) %copy-start.5) | copy-done | bytes 3096
  5.9 0.0 copy-start.6
  5.9 0.7 %copy-done.6 = f32[4,49]{1,0:T(4,128)S(1)} copy-done((f32[4,49]{1,0:T(4,128)S(1)}, f32[4,49]{1,0:T(4,128)}, u32[]{:S(2)}) %copy-start.6) | copy-done | bytes 808
  6.5 0.0 copy-start.7
  6.5 0.7 %copy-done.7 = s32[4,49]{1,0:T(4,128)S(1)} copy-done((s32[4,49]{1,0:T(4,128)S(1)}, s32[4,49]{1,0:T(4,128)}, u32[]{:S(2)}) %copy-start.7) | copy-done | bytes 808
  7.2 0.0 copy-start.8
  7.2 0.7 %copy-done.8 = s32[4,49]{1,0:T(4,128)S(1)} copy-done((s32[4,49]{1,0:T(4,128)S(1)}, s32[4,49]{1,0:T(4,128)}, u32[]{:S(2)}) %copy-start.8) | copy-done | bytes 808
  7.9 0.0 copy-start.9
  7.9 0.7 %copy-done.9 = s32[4]{0:T(128)S(1)} copy-done((s32[4]{0:T(128)S(1)}, s32[4]{0:T(128)}, u32[]{:S(2)}) %copy-start.9) | copy-done | bytes 40
  8.6 37.7 %shard_map.100 = f32[32,512]{1,0:T(8,128)S(1)} custom-call(bf16[4,64,360]{2,1,0:T(8,128)(2,1)S(1)} %bitcast.4, bf16[128,128]{1,0:T(8,128)(2,1)S(1)} %pad_maximum_fusion.weights, f32[4,49]{1,0:T(4,128)S(1)} %copy-done.6, s32[4,49]{1,0:T(4,128)S(1)} %copy-done.7, s32[4,49]{1,0:T(4,128)S(1)} %copy-done.8, s32[4]{0:T(128)S(1)} %copy-done.9, ...), custom_call_target="tpu_custom_call" | custom-call | tf_op jit(solution)/shard_map/pallas_call | solution.py:356
  46.3 0.7 %reshape.7 = f32[1,16,2,2,256]{4,3,2,1,0:T(2,128)} reshape(f32[32,512]{1,0:T(8,128)S(1)} %shard_map.100) | data formatting | bytes 131072 | tf_op jit(solution)/shard_map/reshape | solution.py:397
  (1 shorter events, 0.0 us)
Async XLA Ops:
  0.0 0.9 %copy-start = (bf16[49,64,8]{1,2,0:T(8,128)(2,1)S(1)}, bf16[49,64,8]{1,2,0:T(8,128)(2,1)}, u32[]{:S(2)}) copy-start(bf16[49,64,8]{1,2,0:T(8,128)(2,1)} %param.11) | copy-start | bytes 150532
  1.3 1.4 %copy-start.1 = (bf16[4,360,512]{2,1,0:T(8,128)(2,1)S(1)}, bf16[4,360,512]{2,1,0:T(8,128)(2,1)}, u32[]{:S(2)}) copy-start(bf16[4,360,512]{2,1,0:T(8,128)(2,1)} %constant.20.clone.fourier) | copy-start | bytes 4423684
  2.6 0.9 %copy-start.2 = (bf16[1,4,64,360]{3,2,1,0:T(8,128)(2,1)S(1)}, bf16[1,4,64,360]{3,2,1,0:T(8,128)(2,1)}, u32[]{:S(2)}) copy-start(bf16[1,4,64,360]{3,2,1,0:T(8,128)(2,1)} %param.10) | copy-start | bytes 552964
  3.6 0.9 %copy-start.3 = (bf16[512,128]{1,0:T(8,128)(2,1)S(1)}, bf16[512,128]{1,0:T(8,128)(2,1)}, u32[]{:S(2)}) copy-start(bf16[512,128]{1,0:T(8,128)(2,1)} %constant.21.clone.shift_table) | copy-start | bytes 393220
  4.5 0.7 %copy-start.4 = (f32[3,8,128]{2,1,0:T(8,128)S(1)}, f32[3,8,128]{2,1,0:T(8,128)}, u32[]{:S(2)}) copy-start(f32[3,8,128]{2,1,0:T(8,128)} %constant.22.clone.per_lat) | copy-start | bytes 36868
  5.2 0.7 %copy-start.5 = (f32[768]{0:T(1024)S(1)}, f32[768]{0:T(1024)}, u32[]{:S(2)}) copy-start(f32[768]{0:T(1024)} %constant.23.clone.scalars) | copy-start | bytes 9220
  5.9 0.7 %copy-start.6 = (f32[4,49]{1,0:T(4,128)S(1)}, f32[4,49]{1,0:T(4,128)}, u32[]{:S(2)}) copy-start(f32[4,49]{1,0:T(4,128)} %values.1) | copy-start | bytes 2356
  6.5 0.7 %copy-start.7 = (s32[4,49]{1,0:T(4,128)S(1)}, s32[4,49]{1,0:T(4,128)}, u32[]{:S(2)}) copy-start(s32[4,49]{1,0:T(4,128)} %row_off.1) | copy-start | bytes 2356
  7.2 0.7 %copy-start.8 = (s32[4,49]{1,0:T(4,128)S(1)}, s32[4,49]{1,0:T(4,128)}, u32[]{:S(2)}) copy-start(s32[4,49]{1,0:T(4,128)} %col_off.1) | copy-start | bytes 2356
  7.9 0.7 %copy-start.9 = (s32[4]{0:T(128)S(1)}, s32[4]{0:T(128)}, u32[]{:S(2)}) copy-start(s32[4]{0:T(128)} %sizes.1) | copy-start | bytes 52

commit v2 on v1

--- a/solution.py
+++ b/solution.py
@@ -53,8 +53,9 @@
 
 
 def kernel(
-    fields, weights, values, row_off, col_off, sizes, fourier, shift_table, per_lat, scalars,
+    fields, raw_h, values_h, row_off_h, col_off_h, sizes_h, fourier, shift_table, per_lat_h, scalars_h,
     out,
+    raw, values, row_off, col_off, sizes, per_lat, scalars, wide_w, turned, own_turned, weights,
     blocks, four, shift, xs, meta_v, meta_r, meta_c, left, w, acc, z, send_a, recv_a, wide_a, send_b, recv_b,
     table, tcat,
     sem_in, sem_lon_s, sem_lon_r, sem_halo_s, sem_halo_r, sem_a_s, sem_a_r, sem_b_s, sem_b_r,
@@ -86,14 +87,15 @@
     def _():
         pl.semaphore_signal(barrier, 1, device_id=(lat + 1, lon), device_id_type=MESH)
 
-    get_four = pltpu.make_async_copy(fourier, four, sem_in.at[0])
-    get_shift = pltpu.make_async_copy(shift_table, shift, sem_in.at[1])
-    get_own = pltpu.make_async_copy(
-        fields.at[:, pl.ds(lon * chans, chans), :], blocks.at[lon], sem_in.at[2]
+    own_block = fields.at[:, pl.ds(lon * chans, chans), :]
+    pairs = (
+        (raw_h, raw), (values_h, values), (row_off_h, row_off), (col_off_h, col_off),
+        (sizes_h, sizes), (shift_table, shift), (own_block, blocks.at[lon]), (fourier, four),
+        (per_lat_h, per_lat), (scalars_h, scalars),
     )
-    get_own.start()
-    get_shift.start()
-    get_four.start()
+    fetches = [pltpu.make_async_copy(p, q, sem_in.at[n]) for n, (p, q) in enumerate(pairs)]
+    for fetch in fetches:
+        fetch.start()
 
     common = (lon_parts - 1) + (y_count - 1) + (ZC - 1)
 
@@ -119,6 +121,8 @@
         copy.start()
         lon_copies.append((d, copy))
 
+    for fetch in fetches[:6]:
+        fetch.wait()
     cells = lax.broadcasted_iota(jnp.int32, (1, 2 * HALF), 1) % HALF
     meta_v[...] = jnp.zeros_like(meta_v)
     meta_r[...] = jnp.zeros_like(meta_r)
@@ -127,8 +131,18 @@
         meta_v[:, at : at + SUPPORT] = values[...]
         meta_r[:, at : at + SUPPORT] = row_off[...]
         meta_c[:, at : at + SUPPORT] = col_off[...]
-    get_shift.wait()
-    weights_f32 = weights[...].astype(f32)
+    wide_w[...] = jnp.zeros_like(wide_w)
+    flat = raw[...].astype(f32).reshape(SUPPORT * GROUP, raw.shape[2])
+    for at in (0, HALF * GROUP):
+        wide_w[at : at + SUPPORT * GROUP, : raw.shape[2]] = flat
+    for a in range(GROUP):
+        turned[...] = wide_w[pl.ds(a, 2 * HALF, stride=GROUP), :].T
+        own_turned[a * chans : (a + 1) * chans, :] = turned[
+            pl.ds(pl.multiple_of(lon * chans, chans), chans), :
+        ]
+    for o in range(chans):
+        weights[o * GROUP : (o + 1) * GROUP, :] = own_turned[pl.ds(o, GROUP, stride=chans), :]
+    weights_f32 = weights[...]
     shift_row = lax.broadcasted_iota(jnp.int32, (2 * HALF, 2 * HALF), 0)
     shift_lane = lax.broadcasted_iota(jnp.int32, (2 * HALF, 2 * HALF), 1)
     same_half = shift_row // HALF == shift_lane // HALF
@@ -151,8 +165,8 @@
         part = jnp.dot(data, four[block], preferred_element_type=f32)
         return part.reshape(lat_dev, chans, 2 * deg)
 
-    get_own.wait()
-    get_four.wait()
+    fetches[6].wait()
+    fetches[7].wait()
     own = pl.ds(LAT_REACH, lat_dev)
     xs[own] = transform(lon)
     for d, copy in lon_copies:
@@ -259,6 +273,8 @@
         a_copies.append(copy)
     recv_a[y] = send_a[y]
 
+    fetches[8].wait()
+    fetches[9].wait()
     half = lax.broadcasted_iota(jnp.int32, (8, lat_parts), 0) // lat_dev
     orders = (2 * lat + half).astype(f32)
     order_square = orders * orders
@@ -346,19 +362,25 @@
     _, lat_dev, all_chans, lon_dev = fields.shape
     lat_parts, lon_parts = lax.axis_size("lat"), lax.axis_size("lon")
     chans, deg, y_count = all_chans // lon_parts, 2 * lat_parts, lat_parts // ZC
-    own = lax.dynamic_slice_in_dim(filter_weights, lax.axis_index("lon") * chans, chans, 1)
-    own = own.transpose(1, 2, 0).reshape(chans * GROUP, SUPPORT)
-    own = jnp.pad(own, ((0, 0), (0, HALF - SUPPORT)))
-    own = jnp.concatenate([own, own], axis=1)
-    vmem, smem = pl.BlockSpec(memory_space=pltpu.VMEM), pl.BlockSpec(memory_space=pltpu.SMEM)
-    hbm = pl.BlockSpec(memory_space=pl.ANY)
+    vmem, hbm = pl.BlockSpec(memory_space=pltpu.VMEM), pl.BlockSpec(memory_space=pltpu.HBM)
     f32, bf16, dma = jnp.float32, jnp.bfloat16, pltpu.SemaphoreType.DMA
     result = pl.pallas_call(
         kernel,
         out_shape=jax.ShapeDtypeStruct((chans * 2, 2 * deg), f32),
-        in_specs=[hbm, vmem, vmem, vmem, vmem, smem, hbm, hbm, vmem, smem],
+        in_specs=[hbm] * 10,
         out_specs=vmem,
         scratch_shapes=[
+            pltpu.VMEM((SUPPORT, GROUP, all_chans), bf16),
+            pltpu.VMEM((lat_dev, SUPPORT), f32),
+            pltpu.VMEM((lat_dev, SUPPORT), jnp.int32),
+            pltpu.VMEM((lat_dev, SUPPORT), jnp.int32),
+            pltpu.SMEM((lat_dev,), jnp.int32),
+            pltpu.VMEM((3, 8, lat_parts), f32),
+            pltpu.SMEM((3 * deg,), f32),
+            pltpu.VMEM((2 * HALF * GROUP, 128), f32),
+            pltpu.VMEM((128, 2 * HALF), f32),
+            pltpu.VMEM((chans * GROUP, 2 * HALF), f32),
+            pltpu.VMEM((chans * GROUP, 2 * HALF), f32),
             pltpu.VMEM((lon_parts, lat_dev, chans, lon_dev), bf16),
             pltpu.VMEM((lon_parts, lon_dev, 2 * deg), bf16),
             pltpu.VMEM((2 * deg, 2 * HALF), bf16),
@@ -377,7 +399,7 @@
             pltpu.VMEM((ZC, 2 * y_count, 128), bf16),
             pltpu.VMEM((deg * 8, lat_parts), f32),
             pltpu.VMEM((8, deg, 2 * lat_parts), bf16),
-            dma((3,)),
+            dma((10,)),
             dma((lon_parts - 1,)),
             dma((lon_parts - 1,)),
             dma((2,)),
@@ -388,10 +410,10 @@
             dma((ZC - 1,)),
         ],
         compiler_params=pltpu.CompilerParams(
-            collective_id=0, has_side_effects=True, vmem_limit_bytes=40 * 1024 * 1024
+            collective_id=0, has_side_effects=True, vmem_limit_bytes=60 * 1024 * 1024
         ),
     )(
-        fields[0], own, filter_values, row_offsets, col_offsets, support_sizes,
+        fields[0], filter_weights.transpose(0, 2, 1), filter_values, row_offsets, col_offsets, support_sizes,
         *(jnp.asarray(c) for c in consts),
     )
     return result.reshape(1, chans, 2, 2, deg)

time: 47.3 us -> 39.7 us (0.84)
  local copies, waits for them, and re-layouts: 9.11 us -> 1.51 us
    unnamed x20 -> x0, local copies, waits for them, and re-layouts: 8.18 us -> none
    reshape x1, local copies, waits for them, and re-layouts: 0.67 us -> 1.51 us  [body(): return result.reshape(1, chans, 2, 2, deg)]
where the time goes in v2:
time: 39.7 us; the launch traced here: 39.5 us
  Pallas kernels  38 us (96%)
  local copies, waits for them, and re-layouts  1.51 us (4%)
    pallas_call x1, Pallas kernels, body(): pl.pallas_call(kernel, out_shape=jax.ShapeDtypeStruct((chans * 2, 2 * deg...  38 us
    reshape x1, local copies, waits for them, and re-layouts, body(): return result.reshape(1, chans, 2, 2, deg)  1.51 us

profile of v2, /device:TPU:1, one launch (start us, length us, event | category | flops | bytes accessed | tf_op | source)
XLA Modules:
  0.0 39.5 jit_solution(18189450910524845844)
XLA Ops:
  0.0 38.0 %shard_map.100 = f32[32,512]{1,0:T(8,128)} custom-call(bf16[4,64,360]{2,1,0:T(8,128)(2,1)} %bitcast.2, bf16[49,8,64]{2,1,0:T(8,128)(2,1)} %bitcast.3, f32[4,49]{1,0:T(4,128)} %values_h.1, s32[4,49]{1,0:T(4,128)} %row_off_h.1, s32[4,49]{1,0:T(4,128)} %col_off_h.1, s32[4]{0:T(128)} %sizes_h.1, bf16[4,360,512]{2,1,0:T(8,128)(2,1)} %constant.8.clone.fourier, ...), custom_call_target="tpu_custom_call" | custom-call | tf_op jit(solution)/shard_map/pallas_call | solution.py:367
  38.0 1.5 %reshape.3 = f32[1,16,2,2,256]{4,3,2,1,0:T(2,128)} reshape(f32[32,512]{1,0:T(8,128)} %shard_map.100) | data formatting | bytes 131072 | tf_op jit(solution)/shard_map/reshape | solution.py:419

commit v3 on v2

--- a/solution.py
+++ b/solution.py
@@ -58,7 +58,7 @@
     raw, values, row_off, col_off, sizes, per_lat, scalars, wide_w, turned, own_turned, weights,
     blocks, four, shift, xs, meta_v, meta_r, meta_c, left, w, acc, z, send_a, recv_a, wide_a, send_b, recv_b,
     table, tcat,
-    sem_in, sem_lon_s, sem_lon_r, sem_halo_s, sem_halo_r, sem_a_s, sem_a_r, sem_b_s, sem_b_r,
+    near, far, sem_in, sem_lon_s, sem_lon_r, sem_halo_s, sem_halo_r, sem_a_s, sem_a_r, sem_b_s, sem_b_r,
 ):
     lat, lon = lax.axis_index("lat"), lax.axis_index("lon")
     lat_parts, lon_parts = lax.axis_size("lat"), lax.axis_size("lon")
@@ -68,24 +68,36 @@
     deg = 2 * lat_parts
     f32, bf16 = jnp.float32, jnp.bfloat16
 
+    core, z_at = lat % 2, lat // 2 % (ZC // 2)
+    z_count = ZC // 2
     barrier = pltpu.get_barrier_semaphore()
+    is_low, is_high = core == 0, core == 1
+    has_low, has_high = lat > 0, lat < lat_parts - 1
+    at_end = (lat < lat_parts - 2) & (z_at == z_count - 1)
+    has_before = (lat > 1) & (z_at == 0)
+
+    def tell(sem, to_lat, to_lon):
+        pl.semaphore_signal(sem, 1, device_id=(to_lat, to_lon), device_id_type=MESH)
+
     for d in range(1, lon_parts):
-        pl.semaphore_signal(barrier, 1, device_id=(lat, (lon + d) % lon_parts), device_id_type=MESH)
+        tell(barrier, lat - core, (lon + d) % lon_parts)
+
+    @pl.when(is_high)
+    def _():
+        tell(barrier, lat - 1, lon)
+
     for d in range(1, y_count):
-        pl.semaphore_signal(
-            barrier, 1, device_id=((y + d) % y_count * ZC + zc, lon), device_id_type=MESH
-        )
-    for d in range(1, ZC):
-        pl.semaphore_signal(barrier, 1, device_id=(y * ZC + (zc + d) % ZC, lon), device_id_type=MESH)
-    has_low, has_high = lat > 0, lat < lat_parts - 1
-
-    @pl.when(has_low)
-    def _():
-        pl.semaphore_signal(barrier, 1, device_id=(lat - 1, lon), device_id_type=MESH)
-
-    @pl.when(has_high)
-    def _():
-        pl.semaphore_signal(barrier, 1, device_id=(lat + 1, lon), device_id_type=MESH)
+        tell(barrier, ((y + d) % y_count * z_count + z_at) * 2 + 1, lon)
+    for d in range(1, z_count):
+        tell(barrier, (y * z_count + (z_at + d) % z_count) * 2 + 1, lon)
+
+    @pl.when(has_before)
+    def _():
+        tell(barrier, lat - core - 1, lon)
+
+    @pl.when(at_end)
+    def _():
+        tell(barrier, lat - core + 3, lon)
 
     own_block = fields.at[:, pl.ds(lon * chans, chans), :]
     pairs = (
@@ -97,15 +109,14 @@
     for fetch in fetches:
         fetch.start()
 
-    common = (lon_parts - 1) + (y_count - 1) + (ZC - 1)
-
-    @pl.when(has_low & has_high)
-    def _():
-        pl.semaphore_wait(barrier, common + 2)
-
-    @pl.when(jnp.logical_not(has_low & has_high))
-    def _():
-        pl.semaphore_wait(barrier, common + 1)
+    @pl.when(is_low)
+    def _():
+        pl.semaphore_wait(barrier, 2 * (lon_parts - 1) + 1)
+        tell(near, lat + 1, lon)
+
+    @pl.when(is_high)
+    def _():
+        pl.semaphore_wait(near, 1)
 
     lon_copies = []
     for d in (1, lon_parts - 1, 2):
@@ -190,6 +201,16 @@
         device_id_type=MESH,
     )
 
+    @pl.when(is_high)
+    def _():
+        far_count = 2 * (y_count - 1 + z_count - 1)
+        pl.semaphore_wait(barrier, far_count + 2 * (has_before.astype(jnp.int32) + at_end.astype(jnp.int32)))
+        tell(far, lat - 1, lon)
+
+    @pl.when(is_low)
+    def _():
+        pl.semaphore_wait(far, 1)
+
     @pl.when(has_high)
     def _():
         up.start()
@@ -255,6 +276,14 @@
         return carry
 
     lax.fori_loop(0, lat_dev * groups, other_rows, 0)
+
+    @pl.when(has_high)
+    def _():
+        up.wait_send()
+
+    @pl.when(has_low)
+    def _():
+        down.wait_send()
 
     by_order = z[...].reshape(128, deg).T.astype(bf16)
     send_a[...] = by_order.reshape(y_count, 2 * ZC, 128)
@@ -341,18 +370,10 @@
             part = jnp.concatenate([part, part], axis=1)
             term = lax.dot_general(part, tcat[m * lat_dev + i], NT, preferred_element_type=f32)
             total = term if total is None else total + term
-        out[:, m * deg : (m + 1) * deg] = total
+        out[0, :, :, m, :] = total.reshape(chans, 2, deg)
 
     for _, copy in lon_copies:
         copy.wait_send()
-
-    @pl.when(has_high)
-    def _():
-        up.wait_send()
-
-    @pl.when(has_low)
-    def _():
-        down.wait_send()
 
     for copy in a_copies + b_copies:
         copy.wait_send()
@@ -364,9 +385,9 @@
     chans, deg, y_count = all_chans // lon_parts, 2 * lat_parts, lat_parts // ZC
     vmem, hbm = pl.BlockSpec(memory_space=pltpu.VMEM), pl.BlockSpec(memory_space=pltpu.HBM)
     f32, bf16, dma = jnp.float32, jnp.bfloat16, pltpu.SemaphoreType.DMA
-    result = pl.pallas_call(
+    return pl.pallas_call(
         kernel,
-        out_shape=jax.ShapeDtypeStruct((chans * 2, 2 * deg), f32),
+        out_shape=jax.ShapeDtypeStruct((1, chans, 2, 2, deg), f32),
         in_specs=[hbm] * 10,
         out_specs=vmem,
         scratch_shapes=[
@@ -399,6 +420,8 @@
             pltpu.VMEM((ZC, 2 * y_count, 128), bf16),
             pltpu.VMEM((deg * 8, lat_parts), f32),
             pltpu.VMEM((8, deg, 2 * lat_parts), bf16),
+            pltpu.SemaphoreType.REGULAR,
+            pltpu.SemaphoreType.REGULAR,
             dma((10,)),
             dma((lon_parts - 1,)),
             dma((lon_parts - 1,)),
@@ -416,7 +439,6 @@
         fields[0], filter_weights.transpose(0, 2, 1), filter_values, row_offsets, col_offsets, support_sizes,
         *(jnp.asarray(c) for c in consts),
     )
-    return result.reshape(1, chans, 2, 2, deg)
 
 
 def solution(mesh):

time: 39.7 us -> 36.3 us (0.914)
  Pallas kernels: 38 us -> 34.6 us
    pallas_call x1, Pallas kernels: 38 us -> 34.6 us  [body(): pl.pallas_call(kernel, out_shape=jax.ShapeDtypeStruct((1, chans, 2, 2, de...]
    reshape x1 -> x0, local copies, waits for them, and re-layouts: 1.51 us -> none  [body(): return result.reshape(1, chans, 2, 2, deg)]
    unnamed x0 -> x1, local copies, waits for them, and re-layouts: none -> 1.47 us
where the time goes in v3:
time: 36.3 us; the launch traced here: 36.1 us
  Pallas kernels  34.6 us (95%)
  local copies, waits for them, and re-layouts  1.47 us (4%)
    pallas_call x1, Pallas kernels, body(): pl.pallas_call(kernel, out_shape=jax.ShapeDtypeStruct((1, chans, 2, 2, de...  34.6 us
    unnamed x1, local copies, waits for them, and re-layouts  1.47 us

profile of v3, /device:TPU:1, one launch (start us, length us, event | category | flops | bytes accessed | tf_op | source)
XLA Modules:
  0.0 36.1 jit_solution(12388104162940265010)
XLA Ops:
  0.0 34.6 %shard_map.100 = f32[1,16,2,2,256]{4,3,2,1,0:T(2,128)} custom-call(bf16[4,64,360]{2,1,0:T(8,128)(2,1)} %bitcast.2, bf16[49,8,64]{2,1,0:T(8,128)(2,1)} %bitcast.3, f32[4,49]{1,0:T(4,128)} %values_h.1, s32[4,49]{1,0:T(4,128)} %row_off_h.1, s32[4,49]{1,0:T(4,128)} %col_off_h.1, s32[4]{0:T(128)} %sizes_h.1, bf16[4,360,512]{2,1,0:T(8,128)(2,1)} %constant.8.clone.fourier, ...), custom_call_target="tpu_custom_call" | custom-call | tf_op jit(solution)/shard_map/pallas_call | solution.py:388
  34.7 1.5 %copy.12 = f32[1,16,2,2,256]{4,3,2,1,0:T(2,128)} copy(f32[1,16,2,2,256]{4,3,2,1,0:T(2,128)} %shard_map.100) | data formatting | bytes 131072

commit v4 on v3

--- a/solution.py
+++ b/solution.py
@@ -16,7 +16,7 @@
 LON_REACH = 16
 ROWS = 2 * LAT_REACH + 1
 HALF = 64
-ZC = 16
+Z = 8
 MESH = pl.DeviceIdType.MESH
 NT = (((1,), (1,)), ((), ()))
 
@@ -38,9 +38,8 @@
     turn = np.concatenate([np.cos(turn), np.sin(turn)], 0)
     shift_table = np.zeros((2 * deg, 2 * HALF), ml_dtypes.bfloat16)
     shift_table[:, : shifts.size], shift_table[:, HALF : HALF + shifts.size] = split(turn)
-    y_count = lat_parts // ZC
-    lane = np.arange(lat_parts)
-    band = (lane % y_count) * ZC + lane // y_count
+    lane, chips = np.arange(lat_parts), lat_parts // 2
+    band = (lane % chips) * 2 + lane // chips
     lats = lat_dev * band[None, :] + (np.arange(8) % lat_dev)[:, None]
     colat = math.pi * (lats + 0.5) / nlat
     per_lat = np.stack([np.cos(colat), np.log(np.sin(colat)), math.pi / nlat * np.sin(colat)])
@@ -62,23 +61,29 @@
 ):
     lat, lon = lax.axis_index("lat"), lax.axis_index("lon")
     lat_parts, lon_parts = lax.axis_size("lat"), lax.axis_size("lon")
-    y_count = lat_parts // ZC
-    y, zc = lat // ZC, lat % ZC
+    chips, y_count = lat_parts // 2, lat_parts // (2 * Z)
+    chip, core = lat // 2, lat % 2
+    y, z_at = chip // Z, chip % Z
     lat_dev, chans = blocks.shape[1], blocks.shape[2]
     deg = 2 * lat_parts
     f32, bf16 = jnp.float32, jnp.bfloat16
 
-    core, z_at = lat % 2, lat // 2 % (ZC // 2)
-    z_count = ZC // 2
     barrier = pltpu.get_barrier_semaphore()
     is_low, is_high = core == 0, core == 1
     has_low, has_high = lat > 0, lat < lat_parts - 1
-    at_end = (lat < lat_parts - 2) & (z_at == z_count - 1)
-    has_before = (lat > 1) & (z_at == 0)
 
     def tell(sem, to_lat, to_lon):
         pl.semaphore_signal(sem, 1, device_id=(to_lat, to_lon), device_id_type=MESH)
 
+    def far_chip(dy, dz):
+        return (y + dy) % y_count * Z + (z_at + dz) % Z
+
+    def hops(dy, dz):
+        return min(dy, y_count - dy) + min(dz, Z - dz)
+
+    turns = [(dy, dz) for dy in range(y_count) for dz in range(Z) if dy or dz]
+    turns.sort(key=lambda t: -hops(*t))
+
     for d in range(1, lon_parts):
         tell(barrier, lat - core, (lon + d) % lon_parts)
 
@@ -86,18 +91,13 @@
     def _():
         tell(barrier, lat - 1, lon)
 
-    for d in range(1, y_count):
-        tell(barrier, ((y + d) % y_count * z_count + z_at) * 2 + 1, lon)
-    for d in range(1, z_count):
-        tell(barrier, (y * z_count + (z_at + d) % z_count) * 2 + 1, lon)
-
-    @pl.when(has_before)
-    def _():
-        tell(barrier, lat - core - 1, lon)
-
-    @pl.when(at_end)
-    def _():
-        tell(barrier, lat - core + 3, lon)
+    @pl.when(is_high & has_high)
+    def _():
+        tell(barrier, lat + 1, lon)
+
+    @pl.when(is_low & has_low)
+    def _():
+        tell(barrier, lat - 2, lon)
 
     own_block = fields.at[:, pl.ds(lon * chans, chans), :]
     pairs = (
@@ -111,7 +111,8 @@
 
     @pl.when(is_low)
     def _():
-        pl.semaphore_wait(barrier, 2 * (lon_parts - 1) + 1)
+        sides = has_low.astype(jnp.int32) + (lat < lat_parts - 2).astype(jnp.int32)
+        pl.semaphore_wait(barrier, 2 * (lon_parts - 1) + 1 + sides)
         tell(near, lat + 1, lon)
 
     @pl.when(is_high)
@@ -131,6 +132,16 @@
         )
         copy.start()
         lon_copies.append((d, copy))
+
+    @pl.when(is_low)
+    def _():
+        for turn in turns[0::2]:
+            tell(barrier, far_chip(*turn) * 2 + 1, lon)
+
+    @pl.when(is_high)
+    def _():
+        for turn in turns[1::2]:
+            tell(barrier, far_chip(*turn) * 2 + 1, lon)
 
     for fetch in fetches[:6]:
         fetch.wait()
@@ -168,8 +179,8 @@
                 rows_of == r - LAT_REACH, effective, 0.0
             ).astype(bf16)
         pick = (same_half & (shift_of_row == meta_c[i : i + 1, :])).astype(f32).astype(bf16)
-        turns = jnp.dot(shift[...], pick, preferred_element_type=f32).astype(bf16)
-        w[i] = lax.dot_general(left[...], turns, NT, preferred_element_type=f32)
+        phases = jnp.dot(shift[...], pick, preferred_element_type=f32).astype(bf16)
+        w[i] = lax.dot_general(left[...], phases, NT, preferred_element_type=f32)
 
     def transform(block):
         data = blocks[block].reshape(lat_dev * chans, blocks.shape[3])
@@ -200,16 +211,6 @@
         device_id=((lat + lat_parts - 1) % lat_parts, lon),
         device_id_type=MESH,
     )
-
-    @pl.when(is_high)
-    def _():
-        far_count = 2 * (y_count - 1 + z_count - 1)
-        pl.semaphore_wait(barrier, far_count + 2 * (has_before.astype(jnp.int32) + at_end.astype(jnp.int32)))
-        tell(far, lat - 1, lon)
-
-    @pl.when(is_low)
-    def _():
-        pl.semaphore_wait(far, 1)
 
     @pl.when(has_high)
     def _():
@@ -286,21 +287,31 @@
         down.wait_send()
 
     by_order = z[...].reshape(128, deg).T.astype(bf16)
-    send_a[...] = by_order.reshape(y_count, 2 * ZC, 128)
+    send_a[...] = by_order.reshape(chips, 4, 128)
+
+    @pl.when(is_high)
+    def _():
+        pl.semaphore_wait(barrier, chips - 1)
+        tell(far, lat - 1, lon)
+
+    @pl.when(is_low)
+    def _():
+        pl.semaphore_wait(far, 1)
+
     a_copies = []
-    for d in range(1, y_count):
-        other = (y + d) % y_count
+    for n, turn in enumerate(turns):
+        other = far_chip(*turn)
         copy = pltpu.make_async_remote_copy(
             src_ref=send_a.at[other],
-            dst_ref=recv_a.at[y],
-            send_sem=sem_a_s.at[d - 1],
-            recv_sem=sem_a_r.at[d - 1],
-            device_id=(other * ZC + zc, lon),
+            dst_ref=recv_a.at[chip],
+            send_sem=sem_a_s.at[n],
+            recv_sem=sem_a_r.at[n],
+            device_id=(other * 2 + core, lon),
             device_id_type=MESH,
         )
         copy.start()
         a_copies.append(copy)
-    recv_a[y] = send_a[y]
+    recv_a[chip] = send_a[chip]
 
     fetches[8].wait()
     fetches[9].wait()
@@ -326,43 +337,36 @@
     zeros = cosine * 0.0
     lax.fori_loop(0, deg, advance, (zeros, zeros, zeros, zeros), unroll=8)
 
-    for copy in a_copies:
-        copy.wait_recv()
-
-    wide_a[...] = recv_a[...].astype(f32).reshape(deg, 128)
-    b_copies = []
-    for d in range(ZC):
-        other = (zc + d) % ZC
-        low = wide_a[pl.ds(2 * other, y_count, stride=2 * ZC), :]
-        high = wide_a[pl.ds(2 * other + 1, y_count, stride=2 * ZC), :]
-        tile = jnp.concatenate([low, high], axis=0).astype(bf16)
-        if d == 0:
-            recv_b[zc] = tile
-            continue
-        send_b[other] = tile
-        copy = pltpu.make_async_remote_copy(
-            src_ref=send_b.at[other],
-            dst_ref=recv_b.at[zc],
-            send_sem=sem_b_s.at[d - 1],
-            recv_sem=sem_b_r.at[d - 1],
-            device_id=(y * ZC + other, lon),
-            device_id_type=MESH,
-        )
-        copy.start()
-        b_copies.append(copy)
-
     for s in range(8):
         exact = table[pl.ds(s, deg, stride=8), :]
         high = exact.astype(bf16)
         tcat[s, :, :lat_parts] = high
         tcat[s, :, lat_parts:] = (exact - high.astype(f32)).astype(bf16)
 
-    for copy in b_copies:
+    for copy in a_copies:
+        copy.wait_send()
+    for copy in a_copies:
         copy.wait_recv()
 
-    arrived = recv_b[...].astype(f32)
+    wide_a[...] = recv_a[...].astype(f32).reshape(deg, 128)
+    rows = [wide_a[pl.ds(j, chips, stride=4), :] for j in range(4)]
     for m in range(2):
-        of_order = arrived[:, m * y_count : (m + 1) * y_count, :].reshape(lat_parts, 128)
+        send_b[m] = jnp.where(is_low, rows[2 + m], rows[m]).astype(bf16)
+    swap = pltpu.make_async_remote_copy(
+        src_ref=send_b,
+        dst_ref=recv_b.at[core],
+        send_sem=sem_b_s.at[0],
+        recv_sem=sem_b_r.at[0],
+        device_id=(lat + 1 - 2 * core, lon),
+        device_id_type=MESH,
+    )
+    swap.start()
+    for m in range(2):
+        recv_b[core, m] = jnp.where(is_low, rows[m], rows[2 + m]).astype(bf16)
+    swap.wait_recv()
+
+    for m in range(2):
+        of_order = recv_b[:, m].astype(f32).reshape(lat_parts, 128)
         by_lat = of_order.T.astype(bf16)
         total = None
         for i in range(lat_dev):
@@ -375,14 +379,13 @@
     for _, copy in lon_copies:
         copy.wait_send()
 
-    for copy in a_copies + b_copies:
-        copy.wait_send()
+    swap.wait_send()
 
 
 def body(consts, fields, filter_weights, filter_values, row_offsets, col_offsets, support_sizes):
     _, lat_dev, all_chans, lon_dev = fields.shape
     lat_parts, lon_parts = lax.axis_size("lat"), lax.axis_size("lon")
-    chans, deg, y_count = all_chans // lon_parts, 2 * lat_parts, lat_parts // ZC
+    chans, deg, chips = all_chans // lon_parts, 2 * lat_parts, lat_parts // 2
     vmem, hbm = pl.BlockSpec(memory_space=pltpu.VMEM), pl.BlockSpec(memory_space=pltpu.HBM)
     f32, bf16, dma = jnp.float32, jnp.bfloat16, pltpu.SemaphoreType.DMA
     return pl.pallas_call(
@@ -413,11 +416,11 @@
             pltpu.VMEM((lat_dev, ROWS * chans * GROUP, 2 * deg), f32),
             pltpu.VMEM((lat_dev * chans // GROUP, GROUP * GROUP, 2 * deg), f32),
             pltpu.VMEM((lat_dev * chans // GROUP, 2 * GROUP, deg), f32),
-            pltpu.VMEM((y_count, 2 * ZC, 128), bf16),
-            pltpu.VMEM((y_count, 2 * ZC, 128), bf16),
+            pltpu.VMEM((chips, 4, 128), bf16),
+            pltpu.VMEM((chips, 4, 128), bf16),
             pltpu.VMEM((deg, 128), f32),
-            pltpu.VMEM((ZC, 2 * y_count, 128), bf16),
-            pltpu.VMEM((ZC, 2 * y_count, 128), bf16),
+            pltpu.VMEM((2, chips, 128), bf16),
+            pltpu.VMEM((2, 2, chips, 128), bf16),
             pltpu.VMEM((deg * 8, lat_parts), f32),
             pltpu.VMEM((8, deg, 2 * lat_parts), bf16),
             pltpu.SemaphoreType.REGULAR,
@@ -427,10 +430,10 @@
             dma((lon_parts - 1,)),
             dma((2,)),
             dma((2,)),
-            dma((y_count - 1,)),
-            dma((y_count - 1,)),
-            dma((ZC - 1,)),
-            dma((ZC - 1,)),
+            dma((chips - 1,)),
+            dma((chips - 1,)),
+            dma((1,)),
+            dma((1,)),
         ],
         compiler_params=pltpu.CompilerParams(
             collective_id=0, has_side_effects=True, vmem_limit_bytes=60 * 1024 * 1024

time: 36.3 us -> 37.5 us (1.033)
  Pallas kernels: 34.6 us -> 35.8 us
    pallas_call x1, Pallas kernels: 34.6 us -> 35.8 us  [body(): pl.pallas_call(kernel, out_shape=jax.ShapeDtypeStruct((1, chans, 2, 2, de...]
where the time goes in v4:
time: 37.5 us; the launch traced here: 37.3 us
  Pallas kernels  35.8 us (95%)
  local copies, waits for them, and re-layouts  1.47 us (4%)
    pallas_call x1, Pallas kernels, body(): pl.pallas_call(kernel, out_shape=jax.ShapeDtypeStruct((1, chans, 2, 2, de...  35.8 us
    unnamed x1, local copies, waits for them, and re-layouts  1.47 us

profile of v4, /device:TPU:1, one launch (start us, length us, event | category | flops | bytes accessed | tf_op | source)
XLA Modules:
  0.0 37.3 jit_solution(9452314903287980413)
XLA Ops:
  0.0 35.8 %shard_map.100 = f32[1,16,2,2,256]{4,3,2,1,0:T(2,128)} custom-call(bf16[4,64,360]{2,1,0:T(8,128)(2,1)} %bitcast.2, bf16[49,8,64]{2,1,0:T(8,128)(2,1)} %bitcast.3, f32[4,49]{1,0:T(4,128)} %values_h.1, s32[4,49]{1,0:T(4,128)} %row_off_h.1, s32[4,49]{1,0:T(4,128)} %col_off_h.1, s32[4]{0:T(128)} %sizes_h.1, bf16[4,360,512]{2,1,0:T(8,128)(2,1)} %constant.8.clone.fourier, ...), custom_call_target="tpu_custom_call" | custom-call | tf_op jit(solution)/shard_map/pallas_call | solution.py:391
  35.8 1.5 %copy.12 = f32[1,16,2,2,256]{4,3,2,1,0:T(2,128)} copy(f32[1,16,2,2,256]{4,3,2,1,0:T(2,128)} %shard_map.100) | data formatting | bytes 131072

commit v5 on v3

--- a/solution.py
+++ b/solution.py
@@ -16,9 +16,13 @@
 LON_REACH = 16
 ROWS = 2 * LAT_REACH + 1
 HALF = 64
-ZC = 16
+Z = 8
 MESH = pl.DeviceIdType.MESH
 NT = (((1,), (1,)), ((), ()))
+
+
+def far_first(count):
+    return sorted(range(1, count), key=lambda d: -min(d, count - d))
 
 
 def split(x):
@@ -38,9 +42,8 @@
     turn = np.concatenate([np.cos(turn), np.sin(turn)], 0)
     shift_table = np.zeros((2 * deg, 2 * HALF), ml_dtypes.bfloat16)
     shift_table[:, : shifts.size], shift_table[:, HALF : HALF + shifts.size] = split(turn)
-    y_count = lat_parts // ZC
-    lane = np.arange(lat_parts)
-    band = (lane % y_count) * ZC + lane // y_count
+    y_count, lane = lat_parts // (2 * Z), np.arange(lat_parts)
+    band = (lane % y_count) * 2 * Z + lane // y_count
     lats = lat_dev * band[None, :] + (np.arange(8) % lat_dev)[:, None]
     colat = math.pi * (lats + 0.5) / nlat
     per_lat = np.stack([np.cos(colat), np.log(np.sin(colat)), math.pi / nlat * np.sin(colat)])
@@ -62,56 +65,41 @@
 ):
     lat, lon = lax.axis_index("lat"), lax.axis_index("lon")
     lat_parts, lon_parts = lax.axis_size("lat"), lax.axis_size("lon")
-    y_count = lat_parts // ZC
-    y, zc = lat // ZC, lat % ZC
+    y_count, zc_count = lat_parts // (2 * Z), 2 * Z
+    chip, core, y, zc = lat // 2, lat % 2, lat // zc_count, lat % zc_count
     lat_dev, chans = blocks.shape[1], blocks.shape[2]
     deg = 2 * lat_parts
     f32, bf16 = jnp.float32, jnp.bfloat16
 
-    core, z_at = lat % 2, lat // 2 % (ZC // 2)
-    z_count = ZC // 2
     barrier = pltpu.get_barrier_semaphore()
     is_low, is_high = core == 0, core == 1
     has_low, has_high = lat > 0, lat < lat_parts - 1
-    at_end = (lat < lat_parts - 2) & (z_at == z_count - 1)
-    has_before = (lat > 1) & (z_at == 0)
 
     def tell(sem, to_lat, to_lon):
         pl.semaphore_signal(sem, 1, device_id=(to_lat, to_lon), device_id_type=MESH)
 
+    def ahead(at, step, count):
+        return jnp.where(at + step >= count, at + step - count, at + step)
+
     for d in range(1, lon_parts):
-        tell(barrier, lat - core, (lon + d) % lon_parts)
+        tell(barrier, lat - core, ahead(lon, d, lon_parts))
 
     @pl.when(is_high)
     def _():
         tell(barrier, lat - 1, lon)
 
-    for d in range(1, y_count):
-        tell(barrier, ((y + d) % y_count * z_count + z_at) * 2 + 1, lon)
-    for d in range(1, z_count):
-        tell(barrier, (y * z_count + (z_at + d) % z_count) * 2 + 1, lon)
-
-    @pl.when(has_before)
-    def _():
-        tell(barrier, lat - core - 1, lon)
-
-    @pl.when(at_end)
-    def _():
-        tell(barrier, lat - core + 3, lon)
-
-    own_block = fields.at[:, pl.ds(lon * chans, chans), :]
-    pairs = (
-        (raw_h, raw), (values_h, values), (row_off_h, row_off), (col_off_h, col_off),
-        (sizes_h, sizes), (shift_table, shift), (own_block, blocks.at[lon]), (fourier, four),
-        (per_lat_h, per_lat), (scalars_h, scalars),
-    )
-    fetches = [pltpu.make_async_copy(p, q, sem_in.at[n]) for n, (p, q) in enumerate(pairs)]
-    for fetch in fetches:
-        fetch.start()
+    @pl.when(is_high & has_high)
+    def _():
+        tell(barrier, lat + 1, lon)
+
+    @pl.when(is_low & has_low)
+    def _():
+        tell(barrier, lat - 2, lon)
 
     @pl.when(is_low)
     def _():
-        pl.semaphore_wait(barrier, 2 * (lon_parts - 1) + 1)
+        sides = has_low.astype(jnp.int32) + (lat < lat_parts - 2).astype(jnp.int32)
+        pl.semaphore_wait(barrier, 2 * (lon_parts - 1) + 1 + sides)
         tell(near, lat + 1, lon)
 
     @pl.when(is_high)
@@ -120,7 +108,7 @@
 
     lon_copies = []
     for d in (1, lon_parts - 1, 2):
-        other = (lon + d) % lon_parts
+        other = ahead(lon, d, lon_parts)
         copy = pltpu.make_async_remote_copy(
             src_ref=fields.at[:, pl.ds(other * chans, chans), :],
             dst_ref=blocks.at[lon],
@@ -131,6 +119,26 @@
         )
         copy.start()
         lon_copies.append((d, copy))
+
+    own_block = fields.at[:, pl.ds(lon * chans, chans), :]
+    pairs = (
+        (raw_h, raw), (values_h, values), (row_off_h, row_off), (col_off_h, col_off),
+        (sizes_h, sizes), (shift_table, shift), (own_block, blocks.at[lon]), (fourier, four),
+        (per_lat_h, per_lat), (scalars_h, scalars),
+    )
+    fetches = [pltpu.make_async_copy(p, q, sem_in.at[n]) for n, (p, q) in enumerate(pairs)]
+    for fetch in fetches:
+        fetch.start()
+
+    @pl.when(is_low)
+    def _():
+        for d in far_first(y_count):
+            tell(barrier, ahead(y, d, y_count) * zc_count + zc + 1, lon)
+
+    @pl.when(is_high)
+    def _():
+        for d in far_first(Z):
+            tell(barrier, y * zc_count + ahead(zc, 2 * d, zc_count), lon)
 
     for fetch in fetches[:6]:
         fetch.wait()
@@ -168,8 +176,8 @@
                 rows_of == r - LAT_REACH, effective, 0.0
             ).astype(bf16)
         pick = (same_half & (shift_of_row == meta_c[i : i + 1, :])).astype(f32).astype(bf16)
-        turns = jnp.dot(shift[...], pick, preferred_element_type=f32).astype(bf16)
-        w[i] = lax.dot_general(left[...], turns, NT, preferred_element_type=f32)
+        phases = jnp.dot(shift[...], pick, preferred_element_type=f32).astype(bf16)
+        w[i] = lax.dot_general(left[...], phases, NT, preferred_element_type=f32)
 
     def transform(block):
         data = blocks[block].reshape(lat_dev * chans, blocks.shape[3])
@@ -201,16 +209,6 @@
         device_id_type=MESH,
     )
 
-    @pl.when(is_high)
-    def _():
-        far_count = 2 * (y_count - 1 + z_count - 1)
-        pl.semaphore_wait(barrier, far_count + 2 * (has_before.astype(jnp.int32) + at_end.astype(jnp.int32)))
-        tell(far, lat - 1, lon)
-
-    @pl.when(is_low)
-    def _():
-        pl.semaphore_wait(far, 1)
-
     @pl.when(has_high)
     def _():
         up.start()
@@ -286,16 +284,26 @@
         down.wait_send()
 
     by_order = z[...].reshape(128, deg).T.astype(bf16)
-    send_a[...] = by_order.reshape(y_count, 2 * ZC, 128)
+    send_a[...] = by_order.reshape(y_count, zc_count * 2, 128)
+
+    @pl.when(is_high)
+    def _():
+        pl.semaphore_wait(barrier, y_count - 1 + Z - 1)
+        tell(far, lat - 1, lon)
+
+    @pl.when(is_low)
+    def _():
+        pl.semaphore_wait(far, 1)
+
     a_copies = []
-    for d in range(1, y_count):
-        other = (y + d) % y_count
+    for d in far_first(y_count):
+        other = ahead(y, d, y_count)
         copy = pltpu.make_async_remote_copy(
             src_ref=send_a.at[other],
             dst_ref=recv_a.at[y],
             send_sem=sem_a_s.at[d - 1],
             recv_sem=sem_a_r.at[d - 1],
-            device_id=(other * ZC + zc, lon),
+            device_id=(other * zc_count + zc, lon),
             device_id_type=MESH,
         )
         copy.start()
@@ -326,15 +334,23 @@
     zeros = cosine * 0.0
     lax.fori_loop(0, deg, advance, (zeros, zeros, zeros, zeros), unroll=8)
 
+    for s in range(8):
+        exact = table[pl.ds(s, deg, stride=8), :]
+        high = exact.astype(bf16)
+        tcat[s, :, :lat_parts] = high
+        tcat[s, :, lat_parts:] = (exact - high.astype(f32)).astype(bf16)
+
+    for copy in a_copies:
+        copy.wait_send()
     for copy in a_copies:
         copy.wait_recv()
 
     wide_a[...] = recv_a[...].astype(f32).reshape(deg, 128)
     b_copies = []
-    for d in range(ZC):
-        other = (zc + d) % ZC
-        low = wide_a[pl.ds(2 * other, y_count, stride=2 * ZC), :]
-        high = wide_a[pl.ds(2 * other + 1, y_count, stride=2 * ZC), :]
+    for d in [2 * d + e for d in far_first(Z) for e in (0, 1)] + [1, 0]:
+        other = ahead(zc, d, zc_count)
+        low = wide_a[pl.ds(2 * other, y_count, stride=2 * zc_count), :]
+        high = wide_a[pl.ds(2 * other + 1, y_count, stride=2 * zc_count), :]
         tile = jnp.concatenate([low, high], axis=0).astype(bf16)
         if d == 0:
             recv_b[zc] = tile
@@ -345,18 +361,14 @@
             dst_ref=recv_b.at[zc],
             send_sem=sem_b_s.at[d - 1],
             recv_sem=sem_b_r.at[d - 1],
-            device_id=(y * ZC + other, lon),
+            device_id=(y * zc_count + other, lon),
             device_id_type=MESH,
         )
         copy.start()
         b_copies.append(copy)
 
-    for s in range(8):
-        exact = table[pl.ds(s, deg, stride=8), :]
-        high = exact.astype(bf16)
-        tcat[s, :, :lat_parts] = high
-        tcat[s, :, lat_parts:] = (exact - high.astype(f32)).astype(bf16)
-
+    for _, copy in lon_copies:
+        copy.wait_send()
     for copy in b_copies:
         copy.wait_recv()
 
@@ -372,17 +384,15 @@
             total = term if total is None else total + term
         out[0, :, :, m, :] = total.reshape(chans, 2, deg)
 
-    for _, copy in lon_copies:
-        copy.wait_send()
-
-    for copy in a_copies + b_copies:
+    for copy in b_copies:
         copy.wait_send()
 
 
 def body(consts, fields, filter_weights, filter_values, row_offsets, col_offsets, support_sizes):
     _, lat_dev, all_chans, lon_dev = fields.shape
     lat_parts, lon_parts = lax.axis_size("lat"), lax.axis_size("lon")
-    chans, deg, y_count = all_chans // lon_parts, 2 * lat_parts, lat_parts // ZC
+    chans, deg = all_chans // lon_parts, 2 * lat_parts
+    y_count, zc_count = lat_parts // (2 * Z), 2 * Z
     vmem, hbm = pl.BlockSpec(memory_space=pltpu.VMEM), pl.BlockSpec(memory_space=pltpu.HBM)
     f32, bf16, dma = jnp.float32, jnp.bfloat16, pltpu.SemaphoreType.DMA
     return pl.pallas_call(
@@ -413,11 +423,11 @@
             pltpu.VMEM((lat_dev, ROWS * chans * GROUP, 2 * deg), f32),
             pltpu.VMEM((lat_dev * chans // GROUP, GROUP * GROUP, 2 * deg), f32),
             pltpu.VMEM((lat_dev * chans // GROUP, 2 * GROUP, deg), f32),
-            pltpu.VMEM((y_count, 2 * ZC, 128), bf16),
-            pltpu.VMEM((y_count, 2 * ZC, 128), bf16),
+            pltpu.VMEM((y_count, 2 * zc_count, 128), bf16),
+            pltpu.VMEM((y_count, 2 * zc_count, 128), bf16),
             pltpu.VMEM((deg, 128), f32),
-            pltpu.VMEM((ZC, 2 * y_count, 128), bf16),
-            pltpu.VMEM((ZC, 2 * y_count, 128), bf16),
+            pltpu.VMEM((zc_count, 2 * y_count, 128), bf16),
+            pltpu.VMEM((zc_count, 2 * y_count, 128), bf16),
             pltpu.VMEM((deg * 8, lat_parts), f32),
             pltpu.VMEM((8, deg, 2 * lat_parts), bf16),
             pltpu.SemaphoreType.REGULAR,
@@ -429,8 +439,8 @@
             dma((2,)),
             dma((y_count - 1,)),
             dma((y_count - 1,)),
-            dma((ZC - 1,)),
-            dma((ZC - 1,)),
+            dma((zc_count - 1,)),
+            dma((zc_count - 1,)),
         ],
         compiler_params=pltpu.CompilerParams(
             collective_id=0, has_side_effects=True, vmem_limit_bytes=60 * 1024 * 1024

time: 36.3 us -> 37.6 us (1.036)
  Pallas kernels: 34.6 us -> 35.9 us
    pallas_call x1, Pallas kernels: 34.6 us -> 35.9 us  [body(): pl.pallas_call(kernel, out_shape=jax.ShapeDtypeStruct((1, chans, 2, 2, de...]
where the time goes in v5:
time: 37.6 us; the launch traced here: 37.4 us
  Pallas kernels  35.9 us (95%)
  local copies, waits for them, and re-layouts  1.47 us (4%)
    pallas_call x1, Pallas kernels, body(): pl.pallas_call(kernel, out_shape=jax.ShapeDtypeStruct((1, chans, 2, 2, de...  35.9 us
    unnamed x1, local copies, waits for them, and re-layouts  1.47 us

profile of v5, /device:TPU:1, one launch (start us, length us, event | category | flops | bytes accessed | tf_op | source)
XLA Modules:
  0.0 37.4 jit_solution(7399550433493419615)
XLA Ops:
  0.0 35.9 %shard_map.100 = f32[1,16,2,2,256]{4,3,2,1,0:T(2,128)} custom-call(bf16[4,64,360]{2,1,0:T(8,128)(2,1)} %bitcast.2, bf16[49,8,64]{2,1,0:T(8,128)(2,1)} %bitcast.3, f32[4,49]{1,0:T(4,128)} %values_h.1, s32[4,49]{1,0:T(4,128)} %row_off_h.1, s32[4,49]{1,0:T(4,128)} %col_off_h.1, s32[4]{0:T(128)} %sizes_h.1, bf16[4,360,512]{2,1,0:T(8,128)(2,1)} %constant.8.clone.fourier, ...), custom_call_target="tpu_custom_call" | custom-call | tf_op jit(solution)/shard_map/pallas_call | solution.py:398
  35.9 1.5 %copy.12 = f32[1,16,2,2,256]{4,3,2,1,0:T(2,128)} copy(f32[1,16,2,2,256]{4,3,2,1,0:T(2,128)} %shard_map.100) | data formatting | bytes 131072

commit v6 on v5

--- a/solution.py
+++ b/solution.py
@@ -23,6 +23,10 @@
 
 def far_first(count):
     return sorted(range(1, count), key=lambda d: -min(d, count - d))
+
+
+def corner_first(count):
+    return sorted(range(count), key=lambda t: min(t, count - t))
 
 
 def split(x):
@@ -59,7 +63,7 @@
     fields, raw_h, values_h, row_off_h, col_off_h, sizes_h, fourier, shift_table, per_lat_h, scalars_h,
     out,
     raw, values, row_off, col_off, sizes, per_lat, scalars, wide_w, turned, own_turned, weights,
-    blocks, four, shift, xs, meta_v, meta_r, meta_c, left, w, acc, z, send_a, recv_a, wide_a, send_b, recv_b,
+    blocks, four, shift, edge, beside, xs, meta_v, meta_r, meta_c, left, w, acc, z, send_a, recv_a, wide_a, send_b, recv_b,
     table, tcat,
     near, far, sem_in, sem_lon_s, sem_lon_r, sem_halo_s, sem_halo_r, sem_a_s, sem_a_r, sem_b_s, sem_b_r,
 ):
@@ -192,17 +196,18 @@
         copy.wait_recv()
         xs[own] += transform((lon + lon_parts - d) % lon_parts)
 
+    edge[...] = xs[own].astype(bf16)
     up = pltpu.make_async_remote_copy(
-        src_ref=xs.at[pl.ds(lat_dev, LAT_REACH)],
-        dst_ref=xs.at[pl.ds(0, LAT_REACH)],
+        src_ref=edge.at[pl.ds(lat_dev - LAT_REACH, LAT_REACH)],
+        dst_ref=beside.at[0],
         send_sem=sem_halo_s.at[0],
         recv_sem=sem_halo_r.at[0],
         device_id=((lat + 1) % lat_parts, lon),
         device_id_type=MESH,
     )
     down = pltpu.make_async_remote_copy(
-        src_ref=xs.at[pl.ds(LAT_REACH, LAT_REACH)],
-        dst_ref=xs.at[pl.ds(LAT_REACH + lat_dev, LAT_REACH)],
+        src_ref=edge.at[pl.ds(0, LAT_REACH)],
+        dst_ref=beside.at[1],
         send_sem=sem_halo_s.at[1],
         recv_sem=sem_halo_r.at[1],
         device_id=((lat + lat_parts - 1) % lat_parts, lon),
@@ -216,14 +221,6 @@
     @pl.when(has_low)
     def _():
         down.start()
-
-    @pl.when(jnp.logical_not(has_low))
-    def _():
-        xs[0:LAT_REACH] = jnp.zeros((LAT_REACH,) + xs.shape[1:], f32)
-
-    @pl.when(jnp.logical_not(has_high))
-    def _():
-        xs[LAT_REACH + lat_dev :] = jnp.zeros((LAT_REACH,) + xs.shape[1:], f32)
 
     groups = chans // GROUP
 
@@ -256,10 +253,20 @@
     @pl.when(has_low)
     def _():
         up.wait_recv()
+        xs[:LAT_REACH] = beside[0].astype(f32)
 
     @pl.when(has_high)
     def _():
         down.wait_recv()
+        xs[LAT_REACH + lat_dev :] = beside[1].astype(f32)
+
+    @pl.when(jnp.logical_not(has_low))
+    def _():
+        xs[:LAT_REACH] = jnp.zeros((LAT_REACH,) + xs.shape[1:], f32)
+
+    @pl.when(jnp.logical_not(has_high))
+    def _():
+        xs[LAT_REACH + lat_dev :] = jnp.zeros((LAT_REACH,) + xs.shape[1:], f32)
 
     def other_rows(ig, carry):
         i, g = ig // groups, ig % groups
@@ -295,19 +302,19 @@
     def _():
         pl.semaphore_wait(far, 1)
 
-    a_copies = []
-    for d in far_first(y_count):
-        other = ahead(y, d, y_count)
-        copy = pltpu.make_async_remote_copy(
-            src_ref=send_a.at[other],
+    a_copies = [
+        pltpu.make_async_remote_copy(
+            src_ref=send_a.at[t],
             dst_ref=recv_a.at[y],
-            send_sem=sem_a_s.at[d - 1],
-            recv_sem=sem_a_r.at[d - 1],
-            device_id=(other * zc_count + zc, lon),
+            send_sem=sem_a_s.at[t],
+            recv_sem=sem_a_r.at[y],
+            device_id=(t * zc_count + zc, lon),
             device_id_type=MESH,
         )
-        copy.start()
-        a_copies.append(copy)
+        for t in range(y_count)
+    ]
+    for t in corner_first(y_count):
+        pl.when(t != y)(a_copies[t].start)
     recv_a[y] = send_a[y]
 
     fetches[8].wait()
@@ -340,37 +347,36 @@
         tcat[s, :, :lat_parts] = high
         tcat[s, :, lat_parts:] = (exact - high.astype(f32)).astype(bf16)
 
-    for copy in a_copies:
-        copy.wait_send()
-    for copy in a_copies:
-        copy.wait_recv()
+    for t in range(y_count):
+        pl.when(t != y)(a_copies[t].wait_send)
+    for t in range(y_count):
+        arrival = pltpu.make_async_copy(recv_a.at[t], recv_a.at[t], sem_a_r.at[t])
+        pl.when(t != y)(arrival.wait)
 
     wide_a[...] = recv_a[...].astype(f32).reshape(deg, 128)
-    b_copies = []
-    for d in [2 * d + e for d in far_first(Z) for e in (0, 1)] + [1, 0]:
-        other = ahead(zc, d, zc_count)
-        low = wide_a[pl.ds(2 * other, y_count, stride=2 * zc_count), :]
-        high = wide_a[pl.ds(2 * other + 1, y_count, stride=2 * zc_count), :]
-        tile = jnp.concatenate([low, high], axis=0).astype(bf16)
-        if d == 0:
-            recv_b[zc] = tile
-            continue
-        send_b[other] = tile
-        copy = pltpu.make_async_remote_copy(
-            src_ref=send_b.at[other],
+    b_copies = [
+        pltpu.make_async_remote_copy(
+            src_ref=send_b.at[t],
             dst_ref=recv_b.at[zc],
-            send_sem=sem_b_s.at[d - 1],
-            recv_sem=sem_b_r.at[d - 1],
-            device_id=(y * zc_count + other, lon),
+            send_sem=sem_b_s.at[t],
+            recv_sem=sem_b_r.at[zc],
+            device_id=(y * zc_count + t, lon),
             device_id_type=MESH,
         )
-        copy.start()
-        b_copies.append(copy)
+        for t in range(zc_count)
+    ]
+    for t in [2 * p + e for p in corner_first(Z) for e in (1, 0)]:
+        low = wide_a[pl.ds(2 * t, y_count, stride=2 * zc_count), :]
+        high = wide_a[pl.ds(2 * t + 1, y_count, stride=2 * zc_count), :]
+        send_b[t] = jnp.concatenate([low, high], axis=0).astype(bf16)
+        pl.when(t != zc)(b_copies[t].start)
+    recv_b[zc] = send_b[zc]
 
     for _, copy in lon_copies:
         copy.wait_send()
-    for copy in b_copies:
-        copy.wait_recv()
+    for t in range(zc_count):
+        arrival = pltpu.make_async_copy(recv_b.at[t], recv_b.at[t], sem_b_r.at[t])
+        pl.when(t != zc)(arrival.wait)
 
     arrived = recv_b[...].astype(f32)
     for m in range(2):
@@ -384,8 +390,8 @@
             total = term if total is None else total + term
         out[0, :, :, m, :] = total.reshape(chans, 2, deg)
 
-    for copy in b_copies:
-        copy.wait_send()
+    for t in range(zc_count):
+        pl.when(t != zc)(b_copies[t].wait_send)
 
 
 def body(consts, fields, filter_weights, filter_values, row_offsets, col_offsets, support_sizes):
@@ -415,6 +421,8 @@
             pltpu.VMEM((lon_parts, lat_dev, chans, lon_dev), bf16),
             pltpu.VMEM((lon_parts, lon_dev, 2 * deg), bf16),
             pltpu.VMEM((2 * deg, 2 * HALF), bf16),
+            pltpu.VMEM((lat_dev, chans, 2 * deg), bf16),
+            pltpu.VMEM((2, LAT_REACH, chans, 2 * deg), bf16),
             pltpu.VMEM((lat_dev + 2 * LAT_REACH, chans, 2 * deg), f32),
             pltpu.VMEM((lat_dev, 2 * HALF), f32),
             pltpu.VMEM((lat_dev, 2 * HALF), jnp.int32),
@@ -437,10 +445,10 @@
             dma((lon_parts - 1,)),
             dma((2,)),
             dma((2,)),
-            dma((y_count - 1,)),
-            dma((y_count - 1,)),
-            dma((zc_count - 1,)),
-            dma((zc_count - 1,)),
+            dma((y_count,)),
+            dma((y_count,)),
+            dma((zc_count,)),
+            dma((zc_count,)),
         ],
         compiler_params=pltpu.CompilerParams(
             collective_id=0, has_side_effects=True, vmem_limit_bytes=60 * 1024 * 1024

time: 37.6 us -> 36.4 us (0.968)
  Pallas kernels: 35.9 us -> 34.8 us
    pallas_call x1, Pallas kernels: 35.9 us -> 34.8 us  [body(): pl.pallas_call(kernel, out_shape=jax.ShapeDtypeStruct((1, chans, 2, 2, de...]
where the time goes in v6:
time: 36.4 us; the launch traced here: 36.3 us
  Pallas kernels  34.8 us (96%)
  local copies, waits for them, and re-layouts  1.47 us (4%)
    pallas_call x1, Pallas kernels, body(): pl.pallas_call(kernel, out_shape=jax.ShapeDtypeStruct((1, chans, 2, 2, de...  34.8 us
    unnamed x1, local copies, waits for them, and re-layouts  1.47 us

profile of v6, /device:TPU:1, one launch (start us, length us, event | category | flops | bytes accessed | tf_op | source)
XLA Modules:
  0.0 36.3 jit_solution(8928934008383501024)
XLA Ops:
  0.0 34.8 %shard_map.100 = f32[1,16,2,2,256]{4,3,2,1,0:T(2,128)} custom-call(bf16[4,64,360]{2,1,0:T(8,128)(2,1)} %bitcast.2, bf16[49,8,64]{2,1,0:T(8,128)(2,1)} %bitcast.3, f32[4,49]{1,0:T(4,128)} %values_h.1, s32[4,49]{1,0:T(4,128)} %row_off_h.1, s32[4,49]{1,0:T(4,128)} %col_off_h.1, s32[4]{0:T(128)} %sizes_h.1, bf16[4,360,512]{2,1,0:T(8,128)(2,1)} %constant.8.clone.fourier, ...), custom_call_target="tpu_custom_call" | custom-call | tf_op jit(solution)/shard_map/pallas_call | solution.py:404
  34.8 1.5 %copy.12 = f32[1,16,2,2,256]{4,3,2,1,0:T(2,128)} copy(f32[1,16,2,2,256]{4,3,2,1,0:T(2,128)} %shard_map.100) | data formatting | bytes 131072

commit v7 on v6

--- a/solution.py
+++ b/solution.py
@@ -12,13 +12,17 @@
 
 GROUP = 8
 SUPPORT = 49
-LAT_REACH = 3
 LON_REACH = 16
-ROWS = 2 * LAT_REACH + 1
 HALF = 64
 Z = 8
 MESH = pl.DeviceIdType.MESH
 NT = (((1,), (1,)), ((), ()))
+WIDE = 384
+PAIRS = {
+    0: (0, 1, 2, 3), 1: (0, 1, 2, 3), 2: (0, 1, 2, 3), 3: (0, 1, 2, 3),
+    4: (1, 2, 3), 5: (2, 3), 6: (3,), -1: (0, 1, 2), -2: (0, 1), -3: (0,),
+}
+FIRST = {i: sum(len(PAIRS[q]) for q in list(PAIRS)[:n]) for n, i in enumerate(PAIRS)}
 
 
 def far_first(count):
@@ -46,8 +50,7 @@
     turn = np.concatenate([np.cos(turn), np.sin(turn)], 0)
     shift_table = np.zeros((2 * deg, 2 * HALF), ml_dtypes.bfloat16)
     shift_table[:, : shifts.size], shift_table[:, HALF : HALF + shifts.size] = split(turn)
-    y_count, lane = lat_parts // (2 * Z), np.arange(lat_parts)
-    band = (lane % y_count) * 2 * Z + lane // y_count
+    band = np.arange(lat_parts)
     lats = lat_dev * band[None, :] + (np.arange(8) % lat_dev)[:, None]
     colat = math.pi * (lats + 0.5) / nlat
     per_lat = np.stack([np.cos(colat), np.log(np.sin(colat)), math.pi / nlat * np.sin(colat)])
@@ -63,7 +66,7 @@
     fields, raw_h, values_h, row_off_h, col_off_h, sizes_h, fourier, shift_table, per_lat_h, scalars_h,
     out,
     raw, values, row_off, col_off, sizes, per_lat, scalars, wide_w, turned, own_turned, weights,
-    blocks, four, shift, edge, beside, xs, meta_v, meta_r, meta_c, left, w, acc, z, send_a, recv_a, wide_a, send_b, recv_b,
+    blocks, four, shift, xs, meta, left, w, z, send_a, recv_a, wide_a, send_b, recv_b, wide_b, natural,
     table, tcat,
     near, far, sem_in, sem_lon_s, sem_lon_r, sem_halo_s, sem_halo_r, sem_a_s, sem_a_r, sem_b_s, sem_b_r,
 ):
@@ -146,14 +149,54 @@
 
     for fetch in fetches[:6]:
         fetch.wait()
-    cells = lax.broadcasted_iota(jnp.int32, (1, 2 * HALF), 1) % HALF
-    meta_v[...] = jnp.zeros_like(meta_v)
-    meta_r[...] = jnp.zeros_like(meta_r)
-    meta_c[...] = jnp.zeros_like(meta_c)
+    cells = lax.broadcasted_iota(jnp.int32, (lat_dev, SUPPORT), 1)
+    own_row = lax.broadcasted_iota(jnp.int32, (lat_dev, SUPPORT), 0)
+    size_of = jnp.zeros((lat_dev, SUPPORT), jnp.int32)
+    for i in range(lat_dev):
+        size_of = jnp.where(own_row == i, sizes[i], size_of)
+    live = (cells < size_of).astype(f32)
+    meta[1] = jnp.zeros(meta.shape[1:], f32)
+
+    @pl.when(jnp.logical_not(has_low))
+    def _():
+        meta[0] = jnp.zeros(meta.shape[1:], f32)
+
+    @pl.when(jnp.logical_not(has_high))
+    def _():
+        meta[2] = jnp.zeros(meta.shape[1:], f32)
+
     for at in (0, HALF):
-        meta_v[:, at : at + SUPPORT] = values[...]
-        meta_r[:, at : at + SUPPORT] = row_off[...]
-        meta_c[:, at : at + SUPPORT] = col_off[...]
+        meta[1, 0:4, at : at + SUPPORT] = values[...] * live
+        meta[1, 4:8, at : at + SUPPORT] = row_off[...].astype(f32)
+        meta[1, 8:12, at : at + SUPPORT] = col_off[...].astype(f32)
+    up = pltpu.make_async_remote_copy(
+        src_ref=meta.at[1],
+        dst_ref=meta.at[0],
+        send_sem=sem_halo_s.at[0],
+        recv_sem=sem_halo_r.at[0],
+        device_id=(jnp.where(has_high, lat + 1, 0), lon),
+        device_id_type=MESH,
+    )
+    down = pltpu.make_async_remote_copy(
+        src_ref=meta.at[1],
+        dst_ref=meta.at[2],
+        send_sem=sem_halo_s.at[1],
+        recv_sem=sem_halo_r.at[1],
+        device_id=(jnp.where(has_low, lat - 1, lat_parts - 1), lon),
+        device_id_type=MESH,
+    )
+
+    @pl.when(has_high)
+    def _():
+        up.start()
+
+    @pl.when(has_low)
+    def _():
+        down.start()
+
+    for slot in (2 * lat_dev - 1, 2 * lat_dev):
+        z[slot * 2 : slot * 2 + 2] = jnp.zeros((2,) + z.shape[1:], f32)
+    natural[...] = jnp.zeros_like(natural)
     wide_w[...] = jnp.zeros_like(wide_w)
     flat = raw[...].astype(f32).reshape(SUPPORT * GROUP, raw.shape[2])
     for at in (0, HALF * GROUP):
@@ -169,129 +212,91 @@
     shift_row = lax.broadcasted_iota(jnp.int32, (2 * HALF, 2 * HALF), 0)
     shift_lane = lax.broadcasted_iota(jnp.int32, (2 * HALF, 2 * HALF), 1)
     same_half = shift_row // HALF == shift_lane // HALF
-    shift_of_row = shift_row % HALF - LON_REACH
-    for i in range(lat_dev):
-        live = (cells < sizes[i]).astype(f32)
-        scaled = meta_v[i : i + 1, :] * live
-        effective = (weights_f32 * scaled).astype(bf16).astype(f32)
-        rows_of = meta_r[i : i + 1, :]
-        for r in range(ROWS):
-            left[r * 128 : (r + 1) * 128, :] = jnp.where(
-                rows_of == r - LAT_REACH, effective, 0.0
+    shift_of_row = (shift_row % HALF - LON_REACH).astype(f32)
+
+    def build(i):
+        part, row = 1 + (i // lat_dev), i % lat_dev
+        effective = (weights_f32 * meta[part, row : row + 1, :]).astype(bf16).astype(f32)
+        rows_of = meta[part, 4 + row : 5 + row, :]
+        rows = PAIRS[i]
+        for n, j in enumerate(rows):
+            left[n * 128 : (n + 1) * 128, :] = jnp.where(
+                rows_of == float(j - i), effective, 0.0
             ).astype(bf16)
-        pick = (same_half & (shift_of_row == meta_c[i : i + 1, :])).astype(f32).astype(bf16)
+        shift_by = meta[part, 8 + row : 9 + row, :]
+        pick = (same_half & (shift_of_row == shift_by)).astype(f32).astype(bf16)
         phases = jnp.dot(shift[...], pick, preferred_element_type=f32).astype(bf16)
-        w[i] = lax.dot_general(left[...], phases, NT, preferred_element_type=f32)
+        block = FIRST[i]
+        w[block : block + len(rows)] = lax.dot_general(
+            left[: len(rows) * 128, :], phases, NT, preferred_element_type=f32
+        ).reshape(len(rows), 128, 2 * deg)
 
     def transform(block):
         data = blocks[block].reshape(lat_dev * chans, blocks.shape[3])
         part = jnp.dot(data, four[block], preferred_element_type=f32)
         return part.reshape(lat_dev, chans, 2 * deg)
 
+    for i in range(lat_dev):
+        build(i)
+
+    @pl.when(has_low)
+    def _():
+        up.wait_recv()
+
+    @pl.when(has_high)
+    def _():
+        down.wait_recv()
+
+    for i in PAIRS:
+        if not 0 <= i < lat_dev:
+            build(i)
     fetches[6].wait()
     fetches[7].wait()
-    own = pl.ds(LAT_REACH, lat_dev)
-    xs[own] = transform(lon)
+    xs[...] = transform(lon)
     for d, copy in lon_copies:
         copy.wait_recv()
-        xs[own] += transform((lon + lon_parts - d) % lon_parts)
-
-    edge[...] = xs[own].astype(bf16)
-    up = pltpu.make_async_remote_copy(
-        src_ref=edge.at[pl.ds(lat_dev - LAT_REACH, LAT_REACH)],
-        dst_ref=beside.at[0],
-        send_sem=sem_halo_s.at[0],
-        recv_sem=sem_halo_r.at[0],
-        device_id=((lat + 1) % lat_parts, lon),
-        device_id_type=MESH,
-    )
-    down = pltpu.make_async_remote_copy(
-        src_ref=edge.at[pl.ds(0, LAT_REACH)],
-        dst_ref=beside.at[1],
-        send_sem=sem_halo_s.at[1],
-        recv_sem=sem_halo_r.at[1],
-        device_id=((lat + lat_parts - 1) % lat_parts, lon),
-        device_id_type=MESH,
-    )
+        xs[...] += transform((lon + lon_parts - d) % lon_parts)
+
+    groups = chans // GROUP
+
+    def combine(block, rows, slot, g):
+        part = pl.ds(pl.multiple_of(g * GROUP, GROUP), GROUP)
+        x_rows = [(xs[j, part, :deg], xs[j, part, deg:]) for j in rows]
+        for o in range(GROUP):
+            at = pl.multiple_of(g * (GROUP * GROUP), GROUP * GROUP) + o * GROUP
+            real = imag = None
+            for n, (xr, xi) in enumerate(x_rows):
+                tile = w[block + n, pl.ds(at, GROUP), :]
+                wr, wi = tile[:, :deg], tile[:, deg:]
+                re, im = wr * xr - wi * xi, wr * xi + wi * xr
+                real, imag = (re, im) if real is None else (real + re, imag + im)
+            z[slot * groups + g, 2 * o : 2 * o + 1, :] = jnp.sum(real, axis=0, keepdims=True)
+            z[slot * groups + g, 2 * o + 1 : 2 * o + 2, :] = jnp.sum(imag, axis=0, keepdims=True)
+
+    def own_lats(ig, carry):
+        i, g = ig // groups, ig % groups
+        combine(i * lat_dev, list(range(lat_dev)), i, g)
+        return carry
+
+    def next_lats(g, carry):
+        for i, rows in PAIRS.items():
+            if not 0 <= i < lat_dev:
+                combine(FIRST[i], rows, i if i > 0 else 3 * lat_dev + i, g)
+        return carry
+
+    lax.fori_loop(0, lat_dev * groups, own_lats, 0)
+    lax.fori_loop(0, groups, next_lats, 0)
 
     @pl.when(has_high)
     def _():
-        up.start()
+        up.wait_send()
 
     @pl.when(has_low)
     def _():
-        down.start()
-
-    groups = chans // GROUP
-
-    def products(i, g, o, rows, x_rows):
-        real = imag = None
-        at = pl.multiple_of(g * (GROUP * GROUP), GROUP * GROUP) + o * GROUP
-        for row, (xr, xi) in zip(rows, x_rows):
-            tile = w[i, pl.ds(pl.multiple_of((row - i) * 128 + at, GROUP), GROUP), :]
-            wr, wi = tile[:, :deg], tile[:, deg:]
-            re, im = wr * xr - wi * xi, wr * xi + wi * xr
-            real, imag = (re, im) if real is None else (real + re, imag + im)
-        return real, imag
-
-    def load_rows(rows, g):
-        tiles = [xs[row, pl.ds(pl.multiple_of(g * GROUP, GROUP), GROUP), :] for row in rows]
-        return [(t[:, :deg], t[:, deg:]) for t in tiles]
-
-    def own_rows(ig, carry):
-        i, g = ig // groups, ig % groups
-        rows = [LAT_REACH + j for j in range(lat_dev)]
-        x_rows = load_rows(rows, g)
-        for o in range(GROUP):
-            real, imag = products(i, g, o, rows, x_rows)
-            acc[ig, o * GROUP : (o + 1) * GROUP, :deg] = real
-            acc[ig, o * GROUP : (o + 1) * GROUP, deg:] = imag
-        return carry
-
-    lax.fori_loop(0, lat_dev * groups, own_rows, 0)
-
-    @pl.when(has_low)
-    def _():
-        up.wait_recv()
-        xs[:LAT_REACH] = beside[0].astype(f32)
-
-    @pl.when(has_high)
-    def _():
-        down.wait_recv()
-        xs[LAT_REACH + lat_dev :] = beside[1].astype(f32)
-
-    @pl.when(jnp.logical_not(has_low))
-    def _():
-        xs[:LAT_REACH] = jnp.zeros((LAT_REACH,) + xs.shape[1:], f32)
-
-    @pl.when(jnp.logical_not(has_high))
-    def _():
-        xs[LAT_REACH + lat_dev :] = jnp.zeros((LAT_REACH,) + xs.shape[1:], f32)
-
-    def other_rows(ig, carry):
-        i, g = ig // groups, ig % groups
-        rows = [i + j + lat_dev * ((i + j) // LAT_REACH) for j in range(LAT_REACH)]
-        x_rows = load_rows(rows, g)
-        for o in range(GROUP):
-            real, imag = products(i, g, o, rows, x_rows)
-            real += acc[ig, o * GROUP : (o + 1) * GROUP, :deg]
-            imag += acc[ig, o * GROUP : (o + 1) * GROUP, deg:]
-            z[ig, 2 * o : 2 * o + 1, :] = jnp.sum(real, axis=0, keepdims=True)
-            z[ig, 2 * o + 1 : 2 * o + 2, :] = jnp.sum(imag, axis=0, keepdims=True)
-        return carry
-
-    lax.fori_loop(0, lat_dev * groups, other_rows, 0)
-
-    @pl.when(has_high)
-    def _():
-        up.wait_send()
-
-    @pl.when(has_low)
-    def _():
         down.wait_send()
 
-    by_order = z[...].reshape(128, deg).T.astype(bf16)
-    send_a[...] = by_order.reshape(y_count, zc_count * 2, 128)
+    by_order = z[...].reshape(WIDE, deg).T.astype(bf16)
+    send_a[...] = by_order.reshape(y_count, zc_count * 2, WIDE)
 
     @pl.when(is_high)
     def _():
@@ -353,7 +358,9 @@
         arrival = pltpu.make_async_copy(recv_a.at[t], recv_a.at[t], sem_a_r.at[t])
         pl.when(t != y)(arrival.wait)
 
-    wide_a[...] = recv_a[...].astype(f32).reshape(deg, 128)
+    came_a = recv_a[...].astype(f32).reshape(deg, WIDE)
+    for part in range(3):
+        wide_a[part] = came_a[:, part * 128 : (part + 1) * 128]
     b_copies = [
         pltpu.make_async_remote_copy(
             src_ref=send_b.at[t],
@@ -366,9 +373,12 @@
         for t in range(zc_count)
     ]
     for t in [2 * p + e for p in corner_first(Z) for e in (1, 0)]:
-        low = wide_a[pl.ds(2 * t, y_count, stride=2 * zc_count), :]
-        high = wide_a[pl.ds(2 * t + 1, y_count, stride=2 * zc_count), :]
-        send_b[t] = jnp.concatenate([low, high], axis=0).astype(bf16)
+        for part in range(3):
+            low = wide_a[part, pl.ds(2 * t, y_count, stride=2 * zc_count), :]
+            high = wide_a[part, pl.ds(2 * t + 1, y_count, stride=2 * zc_count), :]
+            send_b[t, :, part * 128 : (part + 1) * 128] = jnp.concatenate(
+                [low, high], axis=0
+            ).astype(bf16)
         pl.when(t != zc)(b_copies[t].start)
     recv_b[zc] = send_b[zc]
 
@@ -378,15 +388,31 @@
         arrival = pltpu.make_async_copy(recv_b.at[t], recv_b.at[t], sem_b_r.at[t])
         pl.when(t != zc)(arrival.wait)
 
-    arrived = recv_b[...].astype(f32)
+    came_b = recv_b[...].astype(f32).reshape(deg, WIDE)
+    for part in range(3):
+        wide_b[part] = came_b[:, part * 128 : (part + 1) * 128]
     for m in range(2):
-        of_order = arrived[:, m * y_count : (m + 1) * y_count, :].reshape(lat_parts, 128)
-        by_lat = of_order.T.astype(bf16)
+        for t in range(y_count):
+            for part in range(3):
+                natural[m, part, 8 + t * zc_count : 8 + (t + 1) * zc_count, :] = wide_b[
+                    part, pl.ds(m * y_count + t, zc_count, stride=2 * y_count), :
+                ]
+        of_order = (
+            natural[m, 0, 8 : 8 + lat_parts, :]
+            + natural[m, 1, 7 : 7 + lat_parts, :]
+            + natural[m, 2, 9 : 9 + lat_parts, :]
+        )
+        by_lat = of_order.T
         total = None
         for i in range(lat_dev):
-            part = by_lat[i * 32 : (i + 1) * 32, :]
-            part = jnp.concatenate([part, part], axis=1)
-            term = lax.dot_general(part, tcat[m * lat_dev + i], NT, preferred_element_type=f32)
+            exact = by_lat[i * 32 : (i + 1) * 32, :]
+            high = exact.astype(bf16)
+            low = (exact - high.astype(f32)).astype(bf16)
+            both, factor = jnp.concatenate([high, high], axis=1), m * lat_dev + i
+            term = lax.dot_general(both, tcat[factor], NT, preferred_element_type=f32)
+            term += lax.dot_general(
+                low, tcat[factor, :, :lat_parts], NT, preferred_element_type=f32
+            )
             total = term if total is None else total + term
         out[0, :, :, m, :] = total.reshape(chans, 2, deg)
 
@@ -421,21 +447,18 @@
             pltpu.VMEM((lon_parts, lat_dev, chans, lon_dev), bf16),
             pltpu.VMEM((lon_parts, lon_dev, 2 * deg), bf16),
             pltpu.VMEM((2 * deg, 2 * HALF), bf16),
-            pltpu.VMEM((lat_dev, chans, 2 * deg), bf16),
-            pltpu.VMEM((2, LAT_REACH, chans, 2 * deg), bf16),
-            pltpu.VMEM((lat_dev + 2 * LAT_REACH, chans, 2 * deg), f32),
-            pltpu.VMEM((lat_dev, 2 * HALF), f32),
-            pltpu.VMEM((lat_dev, 2 * HALF), jnp.int32),
-            pltpu.VMEM((lat_dev, 2 * HALF), jnp.int32),
-            pltpu.VMEM((ROWS * chans * GROUP, 2 * HALF), bf16),
-            pltpu.VMEM((lat_dev, ROWS * chans * GROUP, 2 * deg), f32),
-            pltpu.VMEM((lat_dev * chans // GROUP, GROUP * GROUP, 2 * deg), f32),
-            pltpu.VMEM((lat_dev * chans // GROUP, 2 * GROUP, deg), f32),
-            pltpu.VMEM((y_count, 2 * zc_count, 128), bf16),
-            pltpu.VMEM((y_count, 2 * zc_count, 128), bf16),
-            pltpu.VMEM((deg, 128), f32),
-            pltpu.VMEM((zc_count, 2 * y_count, 128), bf16),
-            pltpu.VMEM((zc_count, 2 * y_count, 128), bf16),
+            pltpu.VMEM((lat_dev, chans, 2 * deg), f32),
+            pltpu.VMEM((3, 16, 2 * HALF), f32),
+            pltpu.VMEM((lat_dev * 128, 2 * HALF), bf16),
+            pltpu.VMEM((28, 128, 2 * deg), f32),
+            pltpu.VMEM((3 * lat_dev * chans // GROUP, 2 * GROUP, deg), f32),
+            pltpu.VMEM((y_count, 2 * zc_count, WIDE), bf16),
+            pltpu.VMEM((y_count, 2 * zc_count, WIDE), bf16),
+            pltpu.VMEM((3, deg, 128), f32),
+            pltpu.VMEM((zc_count, 2 * y_count, WIDE), bf16),
+            pltpu.VMEM((zc_count, 2 * y_count, WIDE), bf16),
+            pltpu.VMEM((3, deg, 128), f32),
+            pltpu.VMEM((2, 3, lat_parts + 16, 128), f32),
             pltpu.VMEM((deg * 8, lat_parts), f32),
             pltpu.VMEM((8, deg, 2 * lat_parts), bf16),
             pltpu.SemaphoreType.REGULAR,

time: 36.4 us -> 36.9 us (1.014)
  Pallas kernels: 34.8 us -> 35.2 us
    pallas_call x1, Pallas kernels: 34.8 us -> 35.2 us  [body(): pl.pallas_call(kernel, out_shape=jax.ShapeDtypeStruct((1, chans, 2, 2, de...]
where the time goes in v7:
time: 36.9 us; the launch traced here: 36.7 us
  Pallas kernels  35.2 us (95%)
  local copies, waits for them, and re-layouts  1.47 us (4%)
    pallas_call x1, Pallas kernels, body(): pl.pallas_call(kernel, out_shape=jax.ShapeDtypeStruct((1, chans, 2, 2, de...  35.2 us
    unnamed x1, local copies, waits for them, and re-layouts  1.47 us

profile of v7, /device:TPU:1, one launch (start us, length us, event | category | flops | bytes accessed | tf_op | source)
XLA Modules:
  0.0 36.7 jit_solution(17590212825073716376)
XLA Ops:
  0.0 35.2 %shard_map.100 = f32[1,16,2,2,256]{4,3,2,1,0:T(2,128)} custom-call(bf16[4,64,360]{2,1,0:T(8,128)(2,1)} %bitcast.2, bf16[49,8,64]{2,1,0:T(8,128)(2,1)} %bitcast.3, f32[4,49]{1,0:T(4,128)} %values_h.1, s32[4,49]{1,0:T(4,128)} %row_off_h.1, s32[4,49]{1,0:T(4,128)} %col_off_h.1, s32[4]{0:T(128)} %sizes_h.1, bf16[4,360,512]{2,1,0:T(8,128)(2,1)} %constant.8.clone.fourier, ...), custom_call_target="tpu_custom_call" | custom-call | tf_op jit(solution)/shard_map/pallas_call | solution.py:430
  35.2 1.5 %copy.12 = f32[1,16,2,2,256]{4,3,2,1,0:T(2,128)} copy(f32[1,16,2,2,256]{4,3,2,1,0:T(2,128)} %shard_map.100) | data formatting | bytes 131072

commit v8 on v7

--- a/solution.py
+++ b/solution.py
@@ -195,7 +195,7 @@
         down.start()
 
     for slot in (2 * lat_dev - 1, 2 * lat_dev):
-        z[slot * 2 : slot * 2 + 2] = jnp.zeros((2,) + z.shape[1:], f32)
+        z[:, slot * 2 : slot * 2 + 2] = jnp.zeros((2, 2) + z.shape[2:], f32)
     natural[...] = jnp.zeros_like(natural)
     wide_w[...] = jnp.zeros_like(wide_w)
     flat = raw[...].astype(f32).reshape(SUPPORT * GROUP, raw.shape[2])
@@ -259,33 +259,56 @@
 
     groups = chans // GROUP
 
-    def combine(block, rows, slot, g):
+    width = deg // 2
+
+    def gather_sums(tiles):
+        place = lax.broadcasted_iota(jnp.int32, tiles[0].shape, 0)
+        for bit in (4, 2, 1):
+            clear = (place // bit) % 2 == 0
+            merged = []
+            for p, q in zip(tiles[:bit], tiles[bit:]):
+                back, forth = pltpu.roll(p, 8 - bit, 0), pltpu.roll(q, bit, 0)
+                merged.append(jnp.where(clear, p, q) + jnp.where(clear, back, forth))
+            tiles = merged
+        return tiles[0]
+
+    def combine(block, rows, slot, g, half):
         part = pl.ds(pl.multiple_of(g * GROUP, GROUP), GROUP)
-        x_rows = [(xs[j, part, :deg], xs[j, part, deg:]) for j in rows]
+        re_at = slice(half * width, (half + 1) * width)
+        im_at = slice(deg + half * width, deg + (half + 1) * width)
+        x_rows = [(xs[j, part, re_at], xs[j, part, im_at]) for j in rows]
+        reals, imags = [], []
         for o in range(GROUP):
-            at = pl.multiple_of(g * (GROUP * GROUP), GROUP * GROUP) + o * GROUP
+            at = pl.ds(pl.multiple_of(g * (GROUP * GROUP), GROUP * GROUP) + o * GROUP, GROUP)
             real = imag = None
             for n, (xr, xi) in enumerate(x_rows):
-                tile = w[block + n, pl.ds(at, GROUP), :]
-                wr, wi = tile[:, :deg], tile[:, deg:]
+                wr, wi = w[block + n, at, re_at], w[block + n, at, im_at]
                 re, im = wr * xr - wi * xi, wr * xi + wi * xr
                 real, imag = (re, im) if real is None else (real + re, imag + im)
-            z[slot * groups + g, 2 * o : 2 * o + 1, :] = jnp.sum(real, axis=0, keepdims=True)
-            z[slot * groups + g, 2 * o + 1 : 2 * o + 2, :] = jnp.sum(imag, axis=0, keepdims=True)
-
-    def own_lats(ig, carry):
-        i, g = ig // groups, ig % groups
-        combine(i * lat_dev, list(range(lat_dev)), i, g)
-        return carry
-
-    def next_lats(g, carry):
-        for i, rows in PAIRS.items():
-            if not 0 <= i < lat_dev:
-                combine(FIRST[i], rows, i if i > 0 else 3 * lat_dev + i, g)
-        return carry
-
-    lax.fori_loop(0, lat_dev * groups, own_lats, 0)
-    lax.fori_loop(0, groups, next_lats, 0)
+            reals.append(real)
+            imags.append(imag)
+        z[half, slot * groups + g, :GROUP, :] = gather_sums(reals)
+        z[half, slot * groups + g, GROUP:, :] = gather_sums(imags)
+
+    def all_lats(half):
+        def own_lats(ig, carry):
+            i, g = ig // groups, ig % groups
+            combine(i * lat_dev, list(range(lat_dev)), i, g, half)
+            return carry
+
+        def next_lats(g, carry):
+            for i, rows in PAIRS.items():
+                if not 0 <= i < lat_dev:
+                    combine(FIRST[i], rows, i if i > 0 else 3 * lat_dev + i, g, half)
+            return carry
+
+        lax.fori_loop(0, lat_dev * groups, own_lats, 0)
+        lax.fori_loop(0, groups, next_lats, 0)
+        by_order = z[half].reshape(WIDE, width).T.astype(bf16)
+        half_y = y_count // 2
+        send_a[half * half_y : (half + 1) * half_y] = by_order.reshape(half_y, zc_count * 2, WIDE)
+
+    all_lats(0)
 
     @pl.when(has_high)
     def _():
@@ -294,9 +317,6 @@
     @pl.when(has_low)
     def _():
         down.wait_send()
-
-    by_order = z[...].reshape(WIDE, deg).T.astype(bf16)
-    send_a[...] = by_order.reshape(y_count, zc_count * 2, WIDE)
 
     @pl.when(is_high)
     def _():
@@ -319,7 +339,12 @@
         for t in range(y_count)
     ]
     for t in corner_first(y_count):
-        pl.when(t != y)(a_copies[t].start)
+        if t < y_count // 2:
+            pl.when(t != y)(a_copies[t].start)
+    all_lats(1)
+    for t in corner_first(y_count):
+        if t >= y_count // 2:
+            pl.when(t != y)(a_copies[t].start)
     recv_a[y] = send_a[y]
 
     fetches[8].wait()
@@ -414,7 +439,10 @@
                 low, tcat[factor, :, :lat_parts], NT, preferred_element_type=f32
             )
             total = term if total is None else total + term
-        out[0, :, :, m, :] = total.reshape(chans, 2, deg)
+        for g in range(groups):
+            for p in range(2):
+                at = (g * 2 + p) * GROUP
+                out[0, g * GROUP : (g + 1) * GROUP, p, m, :] = total[at : at + GROUP, :]
 
     for t in range(zc_count):
         pl.when(t != zc)(b_copies[t].wait_send)
@@ -451,7 +479,7 @@
             pltpu.VMEM((3, 16, 2 * HALF), f32),
             pltpu.VMEM((lat_dev * 128, 2 * HALF), bf16),
             pltpu.VMEM((28, 128, 2 * deg), f32),
-            pltpu.VMEM((3 * lat_dev * chans // GROUP, 2 * GROUP, deg), f32),
+            pltpu.VMEM((2, 3 * lat_dev * chans // GROUP, 2 * GROUP, deg // 2), f32),
             pltpu.VMEM((y_count, 2 * zc_count, WIDE), bf16),
             pltpu.VMEM((y_count, 2 * zc_count, WIDE), bf16),
             pltpu.VMEM((3, deg, 128), f32),

time: 36.9 us -> 35.9 us (0.973)
  the two profiles are of different devices: /device:TPU:1 before, /device:TPU:8 now
where the time goes in v8:
time: 35.9 us; the launch traced here: 35.7 us
  Pallas kernels  34.2 us (95%)
  local copies, waits for them, and re-layouts  1.47 us (4%)
    pallas_call x1, Pallas kernels, body(): pl.pallas_call(kernel, out_shape=jax.ShapeDtypeStruct((1, chans, 2, 2, de...  34.2 us
    unnamed x1, local copies, waits for them, and re-layouts  1.47 us

profile of v8, /device:TPU:8, one launch (start us, length us, event | category | flops | bytes accessed | tf_op | source)
XLA Modules:
  0.0 35.7 jit_solution(15459111845779869546)
XLA Ops:
  0.0 34.2 %shard_map.100 = f32[1,16,2,2,256]{4,3,2,1,0:T(2,128)} custom-call(bf16[4,64,360]{2,1,0:T(8,128)(2,1)} %bitcast.2, bf16[49,8,64]{2,1,0:T(8,128)(2,1)} %bitcast.3, f32[4,49]{1,0:T(4,128)} %values_h.1, s32[4,49]{1,0:T(4,128)} %row_off_h.1, s32[4,49]{1,0:T(4,128)} %col_off_h.1, s32[4]{0:T(128)} %sizes_h.1, bf16[4,360,512]{2,1,0:T(8,128)(2,1)} %constant.8.clone.fourier, ...), custom_call_target="tpu_custom_call" | custom-call | tf_op jit(solution)/shard_map/pallas_call | solution.py:458
  34.2 1.5 %copy.12 = f32[1,16,2,2,256]{4,3,2,1,0:T(2,128)} copy(f32[1,16,2,2,256]{4,3,2,1,0:T(2,128)} %shard_map.100) | data formatting | bytes 131072
